TPU v7x, 128 devices: a whole 4x4x4 slice. The times are simulated.
128 devices in a mesh: req: 32 (over y, z_hi, x), ctx: 4 (over z_lo, core).
Axes of the slice: x: 4, y: 4, z: 4 (z_hi: 2, z_lo: 2; z = z_hi * 2 + z_lo), core: 2. Of those that a mesh axis runs over, the one named last changes fastest.
Arguments:
- queries: bfloat16 [65536, 2048], P(('req', 'ctx')), may hold values from -2.5 to 2.5, as said below
- keys: bfloat16 [65536, 2048], P(('req', 'ctx')), may hold values from -2.5 to 2.5
- values: bfloat16 [65536, 2048], P(('req', 'ctx')), may hold values from -6 to 6
- residual_in: bfloat16 [65536, 4096], P(('req', 'ctx')), may hold values from -4 to 4
- out_weight: bfloat16 [2048, 4096], P('req', 'ctx'), may hold values from -0.75 to 0.75
- lengths: int32 [32], P('req'), may hold values from 256 to 2048
- routes: int32 [4096, 1], P(('req', 'ctx')), may hold values from 0 to 31; in each aligned block of 32 rows (0 to 31, 32 to 63, ...) at most 2 rows name the same one
Outputs:
- memory: bfloat16 [131072, 4096], P(('req', 'ctx'))
Inputs may be any that keep to these rules, and one draw needn't show every extreme that they name: `queries`: hidden draw: some query rows are a multiple of the key row of the same position. `routes`: among the 32 row blocks of one request's position shard, no target appears more than 2 times; in every draw some shard names one target exactly 2 times.
All inputs are finite; a program needn't handle non-finite values.
Results may differ from a plain program's by a relative error of at most 0.012.
Values may be sent and summed in bfloat16 or wider, within the bound.
No kernel may reach another device: no remote copies, remote signals or barrier semaphores. Data moves between devices by JAX's collectives and lax.ppermute only.
A program may use at most 192 MiB of HBM per device.

v0:
```python
import jax
import jax.numpy as jnp
from jax import lax
from jax.sharding import PartitionSpec as P

HEAD_DIM = 256
CAP = 2


NEG_FILL = -1e30


def shards(queries, keys, values, residual_in, out_weight, lengths, routes):
    tok_rows = queries.shape[0]
    width = queries.shape[1]
    head_count = width // HEAD_DIM
    seq_length = lengths[0]
    query_heads = queries.reshape(tok_rows, head_count, HEAD_DIM)
    run_max = jnp.full((tok_rows, head_count), NEG_FILL, jnp.float32)
    key_rows = lax.all_gather(keys, "ctx", axis=0, tiled=True)
    value_rows = lax.all_gather(values, "ctx", axis=0, tiled=True)
    count = key_rows.shape[0]
    key_heads = key_rows.reshape(count, head_count, HEAD_DIM)
    value_heads = value_rows.reshape(count, head_count, HEAD_DIM)
    scores = jnp.einsum("qhe,khe->qhk", query_heads, key_heads, preferred_element_type=jnp.float32)
    valid = jnp.arange(count, dtype=jnp.int32) < seq_length
    scores = jnp.where(valid[None, None, :], scores, NEG_FILL)
    new_max = jnp.maximum(run_max, jnp.max(scores, axis=2))
    weights = jnp.where(valid[None, None, :], jnp.exp(scores - new_max[:, :, None]), 0.0)
    new_sum = jnp.sum(weights, axis=2)
    new_acc = jnp.einsum(
        "qhk,khe->qhe",
        weights.astype(jnp.bfloat16),
        value_heads,
        preferred_element_type=jnp.float32,
    )
    attended = (new_acc / new_sum[:, :, None]).astype(jnp.bfloat16).reshape(tok_rows, width)
    weight_full = lax.all_gather(out_weight, "ctx", axis=1, tiled=True)
    product = jnp.dot(
        attended,
        lax.all_gather(weight_full, "req", axis=0, tiled=True),
        preferred_element_type=jnp.float32,
    )
    encoded = (residual_in.astype(jnp.float32) + product).astype(jnp.bfloat16)
    req_count = lax.axis_size("req")
    block_rows = tok_rows // req_count
    model_width = encoded.shape[1]
    target = routes[:, 0]
    choose = (target[:, None] == jnp.arange(req_count, dtype=jnp.int32)[None, :]).astype(jnp.int32)
    earlier = jnp.cumsum(choose, axis=0) - choose
    slot_index = jnp.sum(earlier * choose, axis=1)
    placed = jnp.zeros((req_count * CAP, block_rows, model_width), jnp.bfloat16)
    placed = placed.at[target * CAP + slot_index].set(
        encoded.reshape(req_count, block_rows, model_width)
    )
    arrived = lax.all_to_all(
        placed.reshape(req_count, CAP * block_rows, model_width),
        "req",
        split_axis=0,
        concat_axis=0,
        tiled=True,
    )
    return arrived.reshape(req_count * CAP * block_rows, model_width)


def solution(mesh):
    return jax.shard_map(
        shards,
        mesh=mesh,
        in_specs=(
            P(("req", "ctx"), None),
            P(("req", "ctx"), None),
            P(("req", "ctx"), None),
            P(("req", "ctx"), None),
            P("req", "ctx"),
            P("req"),
            P(("req", "ctx"), None),
        ),
        out_specs=P(("req", "ctx"), None),
        check_vma=False,
    )
```

profile of v0, /device:TPU:2, one launch (start us, length us, event | category | flops | bytes accessed | tf_op | source)
XLA Modules:
  0.0 488.1 jit_solution(3041723547995714623)
XLA Ops:
  6.5 0.0 copy-start.1
  6.5 0.0 copy-start.2
  6.5 0.0 all-gather.6.cloned.1.call-start
  6.5 0.7 all-gather.6.cloned.1.call-update
  7.3 0.0 all-gather.4.cloned.1.call-start
  7.3 3.9 copy.11
  11.2 0.0 all-gather.4.cloned.1.call-update
  11.3 0.0 all-gather.8.cloned.1.call-start
  11.3 0.0 copy-done.1
  11.3 8.1 %all_gather.14 = bf16[64,4096]{1,0:T(8,128)(2,1)} all-gather(bf16[64,1024]{1,0:T(8,128)(2,1)S(1)} %copy-done.1), channel_id=1, replica_groups=mesh['req'=32,'ctx'=4] {'ctx'}, dimensions={1}, use_global_device_ids=true | all-gather | bytes 655360 | tf_op jit(solution)/shard_map/all_gather | solution.py:38
  19.4 0.0 all-gather.8.cloned.1.call-update
  20.1 0.0 copy-done.2
  20.1 0.1 fusion.17
  20.1 0.1 reduce_window_sum.11
  20.2 0.2 select_reduce_fusion
  20.4 0.0 copy-start
  20.4 71.2 %all-gather.6.cloned.1.call-done = bf16[2048,2048]{1,0:T(8,128)(2,1)} async-done(((bf16[512,2048]{1,0:T(8,128)(2,1)}), bf16[2048,2048]{1,0:T(8,128)(2,1)}) %all-gather.6.cloned.1.call-update) | async-done | bytes 8388624 | tf_op jit(solution)/shard_map/all_gather | solution.py:21
  91.7 12.2 %copy.14 = bf16[2048,2048]{0,1:T(8,128)(2,1)} copy(bf16[2048,2048]{1,0:T(8,128)(2,1)} %all-gather.6.cloned.1.call-done) | data formatting | bytes 16777216 | tf_op jit(solution)/shard_map/all_gather | solution.py:21
  103.9 71.8 %all-gather.4.cloned.1.call-done = bf16[2048,2048]{0,1:T(8,128)(2,1)} async-done(((bf16[512,2048]{0,1:T(8,128)(2,1)}), bf16[2048,2048]{0,1:T(8,128)(2,1)}) %all-gather.4.cloned.1.call-update) | async-done | bytes 8388624 | tf_op jit(solution)/shard_map/all_gather | solution.py:20
  175.7 0.0 copy-done
  175.7 16.7 %bitcast_reduce_fusion = (f32[512,8]{0,1:T(8,128)S(1)}, f32[8,2048,512]{2,1,0:T(8,128)}) fusion(pred[2048]{0:T(1024)(128)(4,1)S(1)} %iota_compare_fusion.1, bf16[2048,8,256]{0,2,1:T(8,128)(2,1)} %bitcast.45, bf16[64,8,8,256]{3,2,1,0:T(8,128)(2,1)S(1)} %bitcast.48), kind=kOutput, calls=%fused_computation.2 | convolution fusion | flops 4311740416 | bytes 44058624 | tf_op jit(solution)/shard_map/qhe,khe->qhk/dot_general | solution.py:25
  192.4 15.0 %fusion.2 = f32[512,8]{0,1:T(8,128)S(1)} fusion(f32[8,2048,512]{2,1,0:T(8,128)} %get-tuple-element.6, f32[512,8]{0,1:T(8,128)S(1)} %broadcast_maximum_fusion, pred[2048]{0:T(1024)(128)(4,1)S(1)} %iota_compare_fusion.1), kind=kLoop, calls=%fused_computation.5 | loop fusion | flops 33550336 | bytes 33589248 | tf_op jit(solution)/shard_map/reduce_sum | solution.py:30
  207.5 18.9 %fusion.11 = bf16[512,8,256]{0,2,1:T(8,128)(2,1)} fusion(bf16[2048,8,256]{0,2,1:T(8,128)(2,1)} %bitcast.46, f32[8,2048,512]{2,1,0:T(8,128)} %get-tuple-element.6, f32[512,8]{0,1:T(8,128)S(1)} %broadcast_maximum_fusion, pred[2048]{0:T(1024)(128)(4,1)S(1)} %iota_compare_fusion.1, f32[512,8]{0,1:T(8,128)S(1)} %fusion.2), kind=kOutput, calls=%fused_computation.15 | convolution fusion | flops 4330618880 | bytes 44075008 | tf_op jit(solution)/shard_map/qhk,khe->qhe/dot_general | solution.py:31
  226.4 111.0 %all-gather.8.cloned.1.call-done = bf16[2048,4096]{1,0:T(8,128)(2,1)} async-done(((bf16[64,4096]{1,0:T(8,128)(2,1)}), bf16[2048,4096]{1,0:T(8,128)(2,1)}) %all-gather.8.cloned.1.call-update) | async-done | bytes 16777232 | tf_op jit(solution)/shard_map/all_gather | solution.py:41
  337.4 17.3 %add_convert_fusion = bf16[512,4096]{1,0:T(8,128)(2,1)} fusion(bf16[512,4096]{1,0:T(8,128)(2,1)} %param.10, bf16[512,2048]{0,1:T(8,128)(2,1)} %bitcast.51, bf16[2048,4096]{1,0:T(8,128)(2,1)} %all-gather.8.cloned.1.call-done), kind=kOutput, calls=%fused_computation.13 | convolution fusion | flops 8596226048 | bytes 27262976 | tf_op jit(solution)/shard_map/dot_general | solution.py:39
  354.7 4.4 broadcast_in_dim.32
  359.1 11.2 %scatter_fusion = bf16[64,16,4096]{2,1,0:T(8,128)(2,1)} fusion(bf16[64,16,4096]{2,1,0:T(8,128)(2,1)} %broadcast_in_dim.32, s32[32]{0:T(128)S(1)} %fusion.18, bf16[32,16,4096]{2,1,0:T(8,128)(2,1)} %bitcast.47), kind=kCustom, calls=%fused_computation | custom fusion | bytes 12583040 | tf_op jit(solution)/shard_map/scatter | solution.py:53
  370.4 103.3 %all_to_all.5 = bf16[32,32,4096]{2,1,0:T(8,128)(2,1)} all-to-all(bf16[32,32,4096]{2,1,0:T(8,128)(2,1)} %bitcast.43), channel_id=1, replica_groups=mesh['req'=32,'ctx'=4] {'req'}, dimensions={0} | all-to-all | bytes 16777216 | tf_op jit(solution)/shard_map/all_to_all | solution.py:56
  473.7 7.9 %copy.28 = bf16[1024,4096]{1,0:T(8,128)(2,1)} copy(bf16[1024,4096]{1,0:T(8,128)(2,1)} %bitcast.44) | data formatting | bytes 16777216
  (3 shorter events, 0.0 us)
Async XLA Ops:
  6.5 4.8 copy-start.1
  6.5 13.5 %copy-start.2 = (s32[32,1]{0,1:T(1,128)S(1)}, s32[32,1]{0,1:T(1,128)}, u32[]{:S(2)}) copy-start(s32[32,1]{0,1:T(1,128)} %param.13) | copy-start | bytes 388
  6.5 85.1 %all-gather.6.cloned.1.call-start = ((), (), s32[]{:S(2)}) async-start(), calls=%async_computation.2 | async-start | bytes 10485760 | tf_op jit(solution)/shard_map/all_gather | solution.py:21
  7.3 168.4 %all-gather.4.cloned.1.call-start = ((), (), s32[]{:S(2)}) async-start(), calls=%async_computation.1 | async-start | bytes 10485760 | tf_op jit(solution)/shard_map/all_gather | solution.py:20
  11.3 326.1 %all-gather.8.cloned.1.call-start = ((), (), s32[]{:S(2)}) async-start(), calls=%async_computation.3 | async-start | bytes 17301504 | tf_op jit(solution)/shard_map/all_gather | solution.py:41
  20.4 155.3 %copy-start = (bf16[512,2048]{1,0:T(8,128)(2,1)S(1)}, bf16[512,2048]{1,0:T(8,128)(2,1)}, u32[]{:S(2)}) copy-start(bf16[512,2048]{1,0:T(8,128)(2,1)} %param.7) | copy-start | bytes 6291460
Sparse Core Ops, SparseCore 0:
  9.0 82.5 all-gather.5
  93.3 82.3 all-gather.3
  178.7 158.6 all-gather.7
where the time goes:
time: 489 us; the launch traced here: 488 us
  waiting for transfers between devices  255 us (52%)
  blocking collectives  111 us (23%)
  matrix products  52.9 us (11%)
  local copies, waits for them, and re-layouts  39.7 us (8%)
  other arithmetic  15.4 us (3%)
  between operations  13.8 us (3%)
    all_gather x1, waiting for transfers between devices, shards(): lax.all_gather(weight_full, 'req', axis=0, tiled=True)  111 us
    all_to_all x1, blocking collectives, shards(): lax.all_to_all(placed.reshape(req_count, CAP * block_rows, model_width),...  103 us
    all_gather x1, waiting for transfers between devices, shards(): key_rows = lax.all_gather(keys, 'ctx', axis=0, tiled=True)  71.8 us
    all_gather x1, waiting for transfers between devices, shards(): value_rows = lax.all_gather(values, 'ctx', axis=0, tiled=True)  71.2 us
    dot_general x1, matrix products, shards(): jnp.einsum('qhk,khe->qhe', weights.astype(jnp.bfloat16), value_heads, pre...  18.9 us
    dot_general x1, matrix products, shards(): jnp.dot(attended, lax.all_gather(weight_full, 'req', axis=0, tiled=True),...  17.3 us
    dot_general x1, matrix products, shards(): jnp.einsum('qhe,khe->qhk', query_heads, key_heads, preferred_element_type...  16.7 us
    reduce_sum x1, other arithmetic, shards(): new_sum = jnp.sum(weights, axis=2)  15 us
  transfers between devices with their start and end apart: 3, of which 3 were waited for; matrix products, arithmetic and copies ran while one was open for 14% of the time, Pallas kernels for 0%

commit v1 on v0

v1 whole, which is shorter than its diff:
```python
import functools

import jax
import jax.numpy as jnp
from jax import lax
from jax.experimental import pallas as pl
from jax.experimental.pallas import tpu as pltpu
from jax.sharding import PartitionSpec as P

HEAD_DIM = 256
CAP = 2
NEG_FILL = -1e30
CHUNKS = (4, 3, 1)
Q_TILE = 256
COL_TILE = 512
MIB = 1024 * 1024


def flip(x, req_bits, ctx_bits):
    req, ctx = lax.axis_size("req"), lax.axis_size("ctx")
    pairs = [
        (r * ctx + c, (r ^ req_bits) * ctx + (c ^ ctx_bits))
        for r in range(req)
        for c in range(ctx)
    ]
    return lax.ppermute(x, ("req", "ctx"), pairs)


def attend_kernel(meta, q, k0, v0, k1, v1, k2, v2, k3, v3, *rest):
    out = rest[-1]
    rows = q.shape[0]
    count = k0.shape[0]
    keys = (k0, k1, k2, k3)
    vals = (v0, v1, v2, v3)
    biases = []
    for i in range(4):
        at = meta[1 + i] + lax.broadcasted_iota(jnp.int32, (1, count), 1)
        biases.append(jnp.where(at < meta[0], 0.0, NEG_FILL).astype(jnp.float32))
    for tile in range(rows // Q_TILE):
        span = slice(tile * Q_TILE, (tile + 1) * Q_TILE)
        rows_q = q[span, :]
        scores = [
            lax.dot_general(
                rows_q,
                keys[i][...],
                (((1,), (1,)), ((), ())),
                preferred_element_type=jnp.float32,
            )
            + biases[i]
            for i in range(4)
        ]
        top = functools.reduce(
            jnp.maximum, [jnp.max(s, axis=1, keepdims=True) for s in scores]
        )
        total = jnp.zeros((Q_TILE, 1), jnp.float32)
        summed = jnp.zeros((Q_TILE, HEAD_DIM), jnp.float32)
        for i in range(4):
            weights = jnp.exp(scores[i] - top)
            total = total + jnp.sum(weights, axis=1, keepdims=True)
            summed = summed + jnp.dot(
                weights.astype(jnp.bfloat16),
                vals[i][...],
                preferred_element_type=jnp.float32,
            )
        out[span, :] = (summed / total).astype(jnp.bfloat16)


def attend(meta, queries, own, beside, far, far_beside, first, heads, before):
    rows = queries.shape[0]
    count = own[0].shape[0]

    def whole(g, meta):
        return (0, first + g)

    def key_of(g, meta):
        return (0, g)

    def value_of(g, meta):
        return (0, heads + g)

    block = lambda n, index: pl.BlockSpec((n, HEAD_DIM), index)
    return pl.pallas_call(
        attend_kernel,
        grid_spec=pltpu.PrefetchScalarGridSpec(
            num_scalar_prefetch=1,
            grid=(heads,),
            in_specs=[block(rows, whole)]
            + [block(count, whole)] * 4
            + [block(count, key_of), block(count, value_of)] * 2
            + [pl.BlockSpec(memory_space=pl.ANY)] * len(before),
            out_specs=block(rows, whole),
        ),
        out_shape=jax.ShapeDtypeStruct(queries.shape, jnp.bfloat16),
        input_output_aliases={10: 0} if before else {},
        compiler_params=pltpu.CompilerParams(vmem_limit_bytes=32 * MIB),
        cost_estimate=pl.CostEstimate(
            flops=0, bytes_accessed=0, transcendentals=0
        ),
    )(meta, queries, *own, *beside, far, far, far_beside, far_beside, *before)


def project_kernel(place, att, source, residual, out, weight):
    core = pl.program_id(2)
    rows = att.shape[0]
    part = source.shape[0] // 64
    for y in range(4):
        for high in range(2):
            for x in range(4):
                to = ((y * 2 + high) * 4 + x) * part
                fro = pl.multiple_of((((y * 4 + x) * 2 + core) * 2 + high) * part, part)
                weight[to : to + part, :] = source[pl.ds(fro, part), :]
    product = jnp.dot(att[...], weight[...], preferred_element_type=jnp.float32)
    encoded = (residual[...].astype(jnp.float32) + product).astype(jnp.bfloat16)
    out[...] = jnp.zeros(out.shape, jnp.bfloat16)
    blocks = place.shape[0]
    block_rows = rows // blocks
    for i in range(blocks):
        to = pl.multiple_of(place[i] * block_rows, block_rows)
        out[pl.ds(to, block_rows), :] = encoded[i * block_rows : (i + 1) * block_rows]


def project(place, attended, weights, residual):
    rows, width = residual.shape
    depth = attended.shape[1]
    tiles = width // 4 // COL_TILE

    def column(low, t, core, place):
        return (0, (low * 2 + core) * tiles + t)

    return pl.pallas_call(
        project_kernel,
        grid_spec=pltpu.PrefetchScalarGridSpec(
            num_scalar_prefetch=1,
            grid=(2, tiles, 2),
            in_specs=[
                pl.BlockSpec(attended.shape, lambda low, t, core, place: (0, 0)),
                pl.BlockSpec(
                    (2 * depth, COL_TILE),
                    lambda low, t, core, place: (0, low * tiles + t),
                ),
                pl.BlockSpec((rows, COL_TILE), column),
            ],
            out_specs=pl.BlockSpec((CAP * rows, COL_TILE), column),
            scratch_shapes=[pltpu.VMEM((depth, COL_TILE), jnp.bfloat16)],
        ),
        out_shape=jax.ShapeDtypeStruct((CAP * rows, width), jnp.bfloat16),
        compiler_params=pltpu.CompilerParams(vmem_limit_bytes=48 * MIB),
        cost_estimate=pl.CostEstimate(
            flops=2 * rows * depth * width,
            bytes_accessed=2 * depth * width + 6 * rows * width,
            transcendentals=0,
        ),
    )(place, attended, weights, residual)


def shards(queries, keys, values, residual_in, out_weight, lengths, routes):
    req, ctx = lax.axis_index("req"), lax.axis_index("ctx")
    low = ctx // 2
    high = lax.rem(req // 4, 2)
    rows = queries.shape[0]
    req_count = lax.axis_size("req")

    packed = []
    first = 0
    for heads in CHUNKS:
        span = slice(first * HEAD_DIM, (first + heads) * HEAD_DIM)
        packed.append(jnp.concatenate([keys[:, span], values[:, span]], axis=1))
        first += heads
    packed[0], out_weight = lax.optimization_barrier((packed[0], out_weight))

    across = flip(out_weight, 0, 2)
    columns = jnp.where(
        low == 0,
        jnp.concatenate([out_weight, across], axis=1),
        jnp.concatenate([across, out_weight], axis=1),
    )
    above = flip(columns, 4, 0)
    pair = jnp.where(
        high == 0,
        jnp.concatenate([columns, above], axis=0),
        jnp.concatenate([above, columns], axis=0),
    )
    planes = [
        [(y * 8 + h * 4 + x) * 4 + z * 2 + k for y in range(4) for x in range(4) for k in range(2)]
        for h in range(2)
        for z in range(2)
    ]
    weights = lax.all_gather(
        pair, ("req", "ctx"), axis=0, tiled=True, axis_index_groups=planes
    )

    beside = (flip(keys, 0, 1), flip(values, 0, 1))
    positions = jnp.stack([(ctx ^ i) * rows for i in range(4)]).astype(jnp.int32)
    meta = jnp.concatenate([lengths, positions])
    attended = ()
    first = 0
    for i, heads in enumerate(CHUNKS):
        far = flip(packed[i], 0, 2)
        if attended:
            far, *attended = lax.optimization_barrier((far, *attended))
        else:
            far, *packed = lax.optimization_barrier((far, *packed))
        far_beside = flip(far, 0, 1)
        done = attend(
            meta, queries, (keys, values), beside, far, far_beside, first, heads, attended
        )
        attended = (done,)
        first += heads

    target = routes[:, 0]
    blocks = target.shape[0]
    order = jnp.arange(blocks, dtype=jnp.int32)
    same = (target[:, None] == target[None, :]) & (order[None, :] < order[:, None])
    cell = target * CAP + jnp.sum(same.astype(jnp.int32), axis=1)

    placed = project(cell, attended[0], weights, residual_in)
    width = placed.shape[1]
    arrived = lax.all_to_all(
        placed.reshape(req_count, -1, width), "req", split_axis=0, concat_axis=0, tiled=True
    )
    return arrived.reshape(-1, width)


def solution(mesh):
    return jax.shard_map(
        shards,
        mesh=mesh,
        in_specs=(
            P(("req", "ctx"), None),
            P(("req", "ctx"), None),
            P(("req", "ctx"), None),
            P(("req", "ctx"), None),
            P("req", "ctx"),
            P("req"),
            P(("req", "ctx"), None),
        ),
        out_specs=P(("req", "ctx"), None),
        check_vma=False,
    )
```

time: 489 us -> 275 us (0.56)
  waiting for transfers between devices: 255 us -> 77.8 us
  matrix products: 52.9 us -> 0 us
  Pallas kernels: 0 us -> 43.1 us
  local copies, waits for them, and re-layouts: 39.7 us -> 17 us
  other arithmetic: 15.4 us -> 4.03 us
  starting transfers between devices: 0.08 us -> 9.59 us
    all_gather x3 -> x1, waiting for transfers between devices: 254 us -> 0.01 us  [shards(): lax.all_gather(pair, ('req', 'ctx'), axis=0, tiled=True, axis_index_group...]
    ppermute x0 -> x10, waiting for transfers between devices: none -> 77.8 us  [flip(): return lax.ppermute(x, ('req', 'ctx'), pairs)]
    dot_general x3 -> x0, matrix products: 52.9 us -> none  [the longest x1 18.9 us: shards(): jnp.einsum('qhk,khe->qhe', weights.astype(jnp.bfloat16), value_heads, pre...]
    pallas_call x0 -> x4, Pallas kernels: none -> 43.1 us  [the longest x3 23.7 us: attend(): pl.pallas_call(attend_kernel, grid_spec=pltpu.PrefetchScalarGridSpec(num_...]
    reduce_sum x2 -> x1, other arithmetic: 15.2 us -> 0.18 us  [shards(): cell = target * CAP + jnp.sum(same.astype(jnp.int32), axis=1)]
    all_gather x1 -> x0, local copies, waits for them, and re-layouts: 12.2 us -> none  [shards(): value_rows = lax.all_gather(values, 'ctx', axis=0, tiled=True)]
    scatter x1 -> x0, local copies, waits for them, and re-layouts: 11.2 us -> none  [shards(): placed.at[target * CAP + slot_index]]
    ppermute x0 -> x10, starting transfers between devices: none -> 9.59 us  [flip(): return lax.ppermute(x, ('req', 'ctx'), pairs)]
  transfers between devices with their start and end apart: 3 -> 11, of which waited for: 3 -> 8; matrix products, arithmetic and copies ran while one was open for 14% -> 1% of each run, Pallas kernels for 0% -> 9%
where the time goes in v1:
time: 275 us; the launch traced here: 274 us
  blocking collectives  109 us (40%)
  waiting for transfers between devices  77.8 us (28%)
  Pallas kernels  43.1 us (16%)
  local copies, waits for them, and re-layouts  17 us (6%)
  between operations  14.2 us (5%)
  starting transfers between devices  9.59 us (3%)
  other arithmetic  4.03 us (1%)
    all_to_all x1, blocking collectives, shards(): lax.all_to_all(placed.reshape(req_count, -1, width), 'req', split_axis=0,...  109 us
    ppermute x10, waiting for transfers between devices, flip(): return lax.ppermute(x, ('req', 'ctx'), pairs)  77.8 us
    pallas_call x3, Pallas kernels, attend(): pl.pallas_call(attend_kernel, grid_spec=pltpu.PrefetchScalarGridSpec(num_...  23.7 us
    pallas_call x1, Pallas kernels, project(): pl.pallas_call(project_kernel, grid_spec=pltpu.PrefetchScalarGridSpec(num...  19.4 us
    unnamed x17, local copies, waits for them, and re-layouts  14.1 us
    ppermute x10, starting transfers between devices, flip(): return lax.ppermute(x, ('req', 'ctx'), pairs)  9.59 us
  transfers between devices with their start and end apart: 11, of which 8 were waited for; matrix products, arithmetic and copies ran while one was open for 1% of the time, Pallas kernels for 9%

profile of v1, /device:TPU:2, one launch (start us, length us, event | category | flops | bytes accessed | tf_op | source)
XLA Modules:
  0.0 274.3 jit_solution(14912427799993060591)
XLA Ops:
  6.5 0.0 slice-start
  6.5 0.0 slice-start.1
  6.5 0.0 all-gather.2.cloned.1.call-start
  6.5 1.2 slice-done
  7.8 0.3 slice-done.1
  8.1 0.0 copy-start.6
  8.1 1.5 pad_maximum_fusion
  9.6 0.0 copy-done.6
  9.6 0.0 copy-start
  9.6 1.9 collective-permute-start.8
  11.5 3.5 %collective-permute-done.8 = bf16[64,1024]{1,0:T(8,128)(2,1)S(1)} collective-permute-done((bf16[64,1024]{1,0:T(8,128)(2,1)S(1)}, bf16[64,1024]{1,0:T(8,128)(2,1)S(1)}, u32[]{:S(2)}, u32[]{:S(2)}) %collective-permute-start.8) | collective-permute-done | bytes 131104 | tf_op jit(solution)/shard_map/ppermute | solution.py:26
  15.0 0.1 maximum_select_fusion.1
  15.1 3.8 %collective-permute-start.9 = (bf16[64,2048]{1,0:T(8,128)(2,1)S(1)}, bf16[64,2048]{1,0:T(8,128)(2,1)S(1)}, u32[]{:S(2)}, u32[]{:S(2)}) collective-permute-start(bf16[64,2048]{1,0:T(8,128)(2,1)S(1)} %maximum_select_fusion.1), channel_id=1, source_target_pairs={{0,16},{1,17},{2,18},{3,19},{4,20},{5,21},{6,22},{7,23},{8,24},{9,... | collective-permute-start | bytes 786440 | tf_op jit(solution)/shard_map/ppermute | solution.py:26
  18.9 5.4 %collective-permute-done.9 = bf16[64,2048]{1,0:T(8,128)(2,1)S(1)} collective-permute-done((bf16[64,2048]{1,0:T(8,128)(2,1)S(1)}, bf16[64,2048]{1,0:T(8,128)(2,1)S(1)}, u32[]{:S(2)}, u32[]{:S(2)}) %collective-permute-start.9) | collective-permute-done | bytes 262176 | tf_op jit(solution)/shard_map/ppermute | solution.py:26
  24.3 0.9 maximum_select_fusion
  25.2 0.0 all-gather.2.cloned.1.call-update
  25.2 0.0 copy-start.1
  25.2 1.4 collective-permute-start.2
  26.6 0.0 copy-done
  26.6 0.0 collective-permute-start
  26.6 0.5 collective-permute-start.1
  27.1 0.1 slice.20
  27.2 1.2 slice.21
  28.4 0.0 copy-done.1
  28.5 1.3 pad_maximum_fusion.1
  29.8 41.6 %collective-permute-done.2.k2.v2 = bf16[512,2048]{1,0:T(8,128)(2,1)} collective-permute-done((bf16[512,2048]{1,0:T(8,128)(2,1)}, bf16[512,2048]{1,0:T(8,128)(2,1)}, u32[]{:S(2)}, u32[]{:S(2)}) %collective-permute-start.2) | collective-permute-done | bytes 2097184 | tf_op jit(solution)/shard_map/ppermute | solution.py:26
  71.5 0.0 collective-permute-start.5
  71.5 1.0 collective-permute-start.4
  73.1 0.1 concatenate.24.meta
  73.2 0.0 collective-permute-done.k1
  73.2 0.0 collective-permute-done.1.v1
  73.2 3.7 %collective-permute-done.5.k3.v3 = bf16[512,2048]{1,0:T(8,128)(2,1)} collective-permute-done((bf16[512,2048]{1,0:T(8,128)(2,1)}, bf16[512,2048]{1,0:T(8,128)(2,1)}, u32[]{:S(2)}, u32[]{:S(2)}) %collective-permute-start.5) | collective-permute-done | bytes 2097184 | tf_op jit(solution)/shard_map/ppermute | solution.py:26
  77.0 0.0 copy-start.2
  77.0 1.6 copy-done.2
  78.6 0.0 copy-start.3
  78.6 1.7 copy-done.3
  80.3 11.3 %shard_map.73.rest_0_ = bf16[512,2048]{1,0:T(8,128)(2,1)S(1)} custom-call(s32[5]{0:T(128)S(1)} %concatenate.24.meta, bf16[512,2048]{1,0:T(8,128)(2,1)S(1)} %copy-done.3, bf16[512,2048]{1,0:T(8,128)(2,1)S(1)} %copy-done, bf16[512,2048]{1,0:T(8,128)(2,1)S(1)} %copy-done.2, bf16[512,2048]{1,0:T(8,128)(2,1)} %collective-permute-done.k1, ...), custom_call_target="tpu_custom_call" | custom-call | tf_op jit(solution)/shard_map/pallas_call | solution.py:82
  91.5 0.0 copy-start.7
  91.6 17.1 %collective-permute-done.4.k2.v2 = bf16[512,1536]{1,0:T(8,128)(2,1)} collective-permute-done((bf16[512,1536]{1,0:T(8,128)(2,1)}, bf16[512,1536]{1,0:T(8,128)(2,1)}, u32[]{:S(2)}, u32[]{:S(2)}) %collective-permute-start.4) | collective-permute-done | bytes 1572896 | tf_op jit(solution)/shard_map/ppermute | solution.py:26
  108.6 0.0 collective-permute-start.6
  108.6 1.0 collective-permute-start.3
  109.6 2.6 collective-permute-done.6.k3.v3
  112.2 8.6 %shard_map.74.rest_0_ = bf16[512,2048]{1,0:T(8,128)(2,1)S(1)} custom-call(s32[5]{0:T(128)S(1)} %concatenate.24.meta, bf16[512,2048]{1,0:T(8,128)(2,1)S(1)} %copy-done.3, bf16[512,2048]{1,0:T(8,128)(2,1)S(1)} %copy-done, bf16[512,2048]{1,0:T(8,128)(2,1)S(1)} %copy-done.2, bf16[512,2048]{1,0:T(8,128)(2,1)} %collective-permute-done.k1, ...), custom_call_target="tpu_custom_call", output_to_operand_aliasing={{}: (10, {})} | custom-call | tf_op jit(solution)/shard_map/pallas_call | solution.py:82
  120.9 2.1 collective-permute-done.3.k2.v2
  123.0 0.0 collective-permute-start.7
  123.0 0.0 copy-done.7
  123.0 0.2 convert_reduce_fusion
  123.1 1.7 collective-permute-done.7.k3.v3
  124.9 3.8 %shard_map.75.att = bf16[512,2048]{1,0:T(8,128)(2,1)S(1)} custom-call(s32[5]{0:T(128)S(1)} %concatenate.24.meta, bf16[512,2048]{1,0:T(8,128)(2,1)S(1)} %copy-done.3, bf16[512,2048]{1,0:T(8,128)(2,1)S(1)} %copy-done, bf16[512,2048]{1,0:T(8,128)(2,1)S(1)} %copy-done.2, bf16[512,2048]{1,0:T(8,128)(2,1)} %collective-permute-done.k1, ...), custom_call_target="tpu_custom_call", output_to_operand_aliasing={{}: (10, {})} | custom-call | tf_op jit(solution)/shard_map/pallas_call | solution.py:82
  128.7 0.0 copy-start.4
  128.7 1.3 copy-done.4
  130.0 0.0 all-gather.2.cloned.1.call-done.source
  130.0 0.0 copy-start.5
  130.0 1.6 copy-done.5
  131.6 19.4 %shard_map.76 = bf16[1024,4096]{1,0:T(8,128)(2,1)} custom-call(s32[32]{0:T(128)S(1)} %multiply_add_fusion.place, bf16[512,2048]{1,0:T(8,128)(2,1)S(1)} %copy-done.5, bf16[4096,2048]{1,0:T(8,128)(2,1)} %all-gather.2.cloned.1.call-done.source, bf16[512,4096]{1,0:T(8,128)(2,1)} %residual.1), custom_call_target="tpu_custom_call" | custom-call | flops 8589934592 | bytes 29360128 | tf_op jit(solution)/shard_map/pallas_call | solution.py:130
  151.0 108.5 %all_to_all.5 = bf16[32,32,4096]{2,1,0:T(8,128)(2,1)} all-to-all(bf16[32,32,4096]{2,1,0:T(8,128)(2,1)} %bitcast.9), channel_id=1, replica_groups=mesh['req'=32,'ctx'=4] {'req'}, dimensions={0} | all-to-all | bytes 16777216 | tf_op jit(solution)/shard_map/all_to_all | solution.py:218
  259.5 7.9 %copy.14 = bf16[1024,4096]{1,0:T(8,128)(2,1)} copy(bf16[1024,4096]{1,0:T(8,128)(2,1)} %bitcast.8) | data formatting | bytes 16777216
  (4 shorter events, 0.1 us)
Async XLA Ops:
  6.5 1.2 slice-start
  6.5 1.5 slice-start.1
  6.5 123.5 %all-gather.2.cloned.1.call-start = ((), (), s32[]{:S(2)}) async-start(), calls=%async_computation.1 | async-start | bytes 17301504 | tf_op jit(solution)/shard_map/all_gather | solution.py:188
  8.1 1.5 copy-start.6
  9.6 17.0 %copy-start = (bf16[512,2048]{1,0:T(8,128)(2,1)S(1)}, bf16[512,2048]{1,0:T(8,128)(2,1)}, u32[]{:S(2)}) copy-start(bf16[512,2048]{1,0:T(8,128)(2,1)} %k0.5) | copy-start | bytes 6291460
  9.6 5.4 %collective-permute-start.8 = (bf16[64,1024]{1,0:T(8,128)(2,1)S(1)}, bf16[64,1024]{1,0:T(8,128)(2,1)S(1)}, u32[]{:S(2)}, u32[]{:S(2)}) collective-permute-start(bf16[64,1024]{1,0:T(8,128)(2,1)S(1)} %copy-done.6), channel_id=1, source_target_pairs={{0,2},{1,3},{2,0},{3,1},{4,6},{5,7},{6,4},{7,5},{8,10},{9,11},{10,... | collective-permute-start | bytes 393224 | tf_op jit(solution)/shard_map/ppermute | solution.py:26
  15.1 9.2 %collective-permute-start.9 = (bf16[64,2048]{1,0:T(8,128)(2,1)S(1)}, bf16[64,2048]{1,0:T(8,128)(2,1)S(1)}, u32[]{:S(2)}, u32[]{:S(2)}) collective-permute-start(bf16[64,2048]{1,0:T(8,128)(2,1)S(1)} %maximum_select_fusion.1), channel_id=1, source_target_pairs={{0,16},{1,17},{2,18},{3,19},{4,20},{5,21},{6,22},{7,23},{8,24},{9,... | collective-permute-start | bytes 786440 | tf_op jit(solution)/shard_map/ppermute | solution.py:26
  25.2 3.2 %copy-start.1 = (bf16[512,2048]{1,0:T(8,128)(2,1)S(1)}, bf16[512,2048]{1,0:T(8,128)(2,1)}, u32[]{:S(2)}) copy-start(bf16[512,2048]{1,0:T(8,128)(2,1)} %v0.5) | copy-start | bytes 6291460
  25.2 46.3 %collective-permute-start.2 = (bf16[512,2048]{1,0:T(8,128)(2,1)}, bf16[512,2048]{1,0:T(8,128)(2,1)}, u32[]{:S(2)}, u32[]{:S(2)}) collective-permute-start(bf16[512,2048]{1,0:T(8,128)(2,1)} %pad_maximum_fusion), channel_id=1, source_target_pairs={{0,2},{1,3},{2,0},{3,1},{4,6},{5,7},{6,4},{7,5},{8,10},{9,11},{10,... | collective-permute-start | bytes 6291464 | tf_op jit(solution)/shard_map/ppermute | solution.py:26
  26.6 46.6 %collective-permute-start = (bf16[512,2048]{1,0:T(8,128)(2,1)S(1)}, bf16[512,2048]{1,0:T(8,128)(2,1)}, u32[]{:S(2)}, u32[]{:S(2)}) collective-permute-start(bf16[512,2048]{1,0:T(8,128)(2,1)S(1)} %copy-done), channel_id=1, source_target_pairs={{0,1},{1,0},{2,3},{3,2},{4,5},{5,4},{6,7},{7,6},{8,9},{9,8},{10,11... | collective-permute-start | bytes 6291464 | tf_op jit(solution)/shard_map/ppermute | solution.py:26
  26.6 46.6 %collective-permute-start.1 = (bf16[512,2048]{1,0:T(8,128)(2,1)}, bf16[512,2048]{1,0:T(8,128)(2,1)}, u32[]{:S(2)}, u32[]{:S(2)}) collective-permute-start(bf16[512,2048]{1,0:T(8,128)(2,1)} %v0.5), channel_id=1, source_target_pairs={{0,1},{1,0},{2,3},{3,2},{4,5},{5,4},{6,7},{7,6},{8,9},{9,8},{10,11... | collective-permute-start | bytes 6291464 | tf_op jit(solution)/shard_map/ppermute | solution.py:26
  71.5 5.5 %collective-permute-start.5 = (bf16[512,2048]{1,0:T(8,128)(2,1)}, bf16[512,2048]{1,0:T(8,128)(2,1)}, u32[]{:S(2)}, u32[]{:S(2)}) collective-permute-start(bf16[512,2048]{1,0:T(8,128)(2,1)} %collective-permute-done.2.k2.v2), channel_id=1, source_target_pairs={{0,1},{1,0},{2,3},{3,2},{4,5},{5,4},{6,7},{7,6},{8,9},{9,8},{10,11... | collective-permute-start | bytes 6291464 | tf_op jit(solution)/shard_map/ppermute | solution.py:26
  71.5 37.1 %collective-permute-start.4 = (bf16[512,1536]{1,0:T(8,128)(2,1)}, bf16[512,1536]{1,0:T(8,128)(2,1)}, u32[]{:S(2)}, u32[]{:S(2)}) collective-permute-start(bf16[512,1536]{1,0:T(8,128)(2,1)} %pad_maximum_fusion.1), channel_id=1, source_target_pairs={{0,2},{1,3},{2,0},{3,1},{4,6},{5,7},{6,4},{7,5},{8,10},{9,11},{10,... | collective-permute-start | bytes 4718600 | tf_op jit(solution)/shard_map/ppermute | solution.py:26
  77.0 1.6 copy-start.2
  78.6 1.7 copy-start.3
  91.5 31.4 %copy-start.7 = (s32[32,1]{0,1:T(1,128)S(1)}, s32[32,1]{0,1:T(1,128)}, u32[]{:S(2)}) copy-start(s32[32,1]{0,1:T(1,128)} %param.13) | copy-start | bytes 388
  108.6 3.6 %collective-permute-start.6 = (bf16[512,1536]{1,0:T(8,128)(2,1)}, bf16[512,1536]{1,0:T(8,128)(2,1)S(1)}, u32[]{:S(2)}, u32[]{:S(2)}) collective-permute-start(bf16[512,1536]{1,0:T(8,128)(2,1)} %collective-permute-done.4.k2.v2), channel_id=1, source_target_pairs={{0,1},{1,0},{2,3},{3,2},{4,5},{5,4},{6,7},{7,6},{8,9},{9,8},{10,11... | collective-permute-start | bytes 4718600 | tf_op jit(solution)/shard_map/ppermute | solution.py:26
  108.6 14.3 %collective-permute-start.3 = (bf16[512,512]{1,0:T(8,128)(2,1)S(1)}, bf16[512,512]{1,0:T(8,128)(2,1)S(1)}, u32[]{:S(2)}, u32[]{:S(2)}) collective-permute-start(bf16[512,512]{1,0:T(8,128)(2,1)S(1)} %pad_maximum_fusion.2), channel_id=1, source_target_pairs={{0,2},{1,3},{2,0},{3,1},{4,6},{5,7},{6,4},{7,5},{8,10},{9,11},{10,... | collective-permute-start | bytes 1572872 | tf_op jit(solution)/shard_map/ppermute | solution.py:26
  123.0 1.9 collective-permute-start.7
  128.7 1.3 copy-start.4
  130.0 1.6 copy-start.5
Sparse Core Ops, SparseCore 0:
  25.3 74.0 all-gather.1

commit v2 on v1

v2 whole, which is shorter than its diff:
```python
import functools

import jax
import jax.numpy as jnp
from jax import lax
from jax.experimental import pallas as pl
from jax.experimental.pallas import tpu as pltpu
from jax.sharding import PartitionSpec as P

HEAD_DIM = 256
CAP = 2
NEG_FILL = -1e30
CHUNKS = (1, 4, 2, 1)
Q_TILE = 256
COL_TILE = 512
ROW_TILE = 512
SLOTS = 3
MIB = 1024 * 1024


def flip(x, req_bits, ctx_bits):
    req, ctx = lax.axis_size("req"), lax.axis_size("ctx")
    pairs = [
        (r * ctx + c, (r ^ req_bits) * ctx + (c ^ ctx_bits))
        for r in range(req)
        for c in range(ctx)
    ]
    return lax.ppermute(x, ("req", "ctx"), pairs)


def attend_head(meta, q, keys, vals, out):
    count = keys[0].shape[0]
    biases = []
    for i in range(4):
        at = meta[1 + i] + lax.broadcasted_iota(jnp.int32, (1, count), 1)
        biases.append(jnp.where(at < meta[0], 0.0, NEG_FILL).astype(jnp.float32))
    for tile in range(q.shape[0] // Q_TILE):
        span = slice(tile * Q_TILE, (tile + 1) * Q_TILE)
        rows_q = q[span, :]
        scores = [
            lax.dot_general(
                rows_q,
                keys[i][...],
                (((1,), (1,)), ((), ())),
                preferred_element_type=jnp.float32,
            )
            + biases[i]
            for i in range(4)
        ]
        top = functools.reduce(
            jnp.maximum, [jnp.max(s, axis=1, keepdims=True) for s in scores]
        )
        total = jnp.zeros((Q_TILE, 1), jnp.float32)
        summed = jnp.zeros((Q_TILE, HEAD_DIM), jnp.float32)
        for i in range(4):
            weights = jnp.exp(scores[i] - top)
            total = total + jnp.sum(weights, axis=1, keepdims=True)
            summed = summed + jnp.dot(
                weights.astype(jnp.bfloat16),
                vals[i][...],
                preferred_element_type=jnp.float32,
            )
        out[span, :] = (summed / total).astype(jnp.bfloat16)


def attend_kernel(meta, q, k0, v0, k1, v1, k2, v2, k3, v3, out):
    attend_head(meta, q, (k0, k1, k2, k3), (v0, v1, v2, v3), out)


def attend(meta, queries, own, beside, far, far_beside, first, heads):
    rows = queries.shape[0]
    count = own[0].shape[0]

    def whole(g, meta):
        return (0, first + g)

    def key_of(g, meta):
        return (0, g)

    def value_of(g, meta):
        return (0, heads + g)

    block = lambda n, index: pl.BlockSpec((n, HEAD_DIM), index)
    return pl.pallas_call(
        attend_kernel,
        grid_spec=pltpu.PrefetchScalarGridSpec(
            num_scalar_prefetch=1,
            grid=(heads,),
            in_specs=[block(rows, whole)]
            + [block(count, whole)] * 4
            + [block(count, key_of), block(count, value_of)] * 2,
            out_specs=block(rows, key_of),
        ),
        out_shape=jax.ShapeDtypeStruct((rows, heads * HEAD_DIM), jnp.bfloat16),
        compiler_params=pltpu.CompilerParams(vmem_limit_bytes=20 * MIB),
        cost_estimate=pl.CostEstimate(
            flops=0, bytes_accessed=0, transcendentals=0
        ),
    )(meta, queries, *own, *beside, far, far, far_beside, far_beside)


def finish_kernel(meta, place, q, near, near_beside, far, far_beside, *refs):
    *parts, weights, residual, out, att, held, sems = refs
    step = pl.program_id(0)
    rows, depth = att.shape
    tiles = weights.shape[-1] // 4 // COL_TILE

    def spot(head):
        at = (head % 2 * 4 + head // 2) * HEAD_DIM
        return slice(at, at + HEAD_DIM)

    def fetch(tile, high):
        low, t, core = tile // (2 * tiles), tile // 2 % tiles, tile % 2
        columns = pl.ds(((high * 2 + low) * tiles + t) * COL_TILE, COL_TILE)
        return pltpu.make_async_copy(
            weights.at[:, :, core, :, columns],
            held.at[tile % SLOTS, high],
            sems.at[tile % SLOTS, high],
        )

    @pl.when(step == 0)
    def _():
        for tile in range(SLOTS - 1):
            for high in range(2):
                fetch(tile, high).start()
        half = slice(0, HEAD_DIM), slice(HEAD_DIM, 2 * HEAD_DIM)
        pieces = (near, near_beside, far, far_beside)
        keys = [piece.at[:, half[0]] for piece in pieces]
        vals = [piece.at[:, half[1]] for piece in pieces]
        head = 0
        for part in parts:
            for i in range(part.shape[1] // HEAD_DIM):
                att[:, spot(head)] = part[:, i * HEAD_DIM : (i + 1) * HEAD_DIM]
                head += 1
        attend_head(meta, q, keys, vals, att.at[:, spot(head)])

    for tile in range(4 * tiles):

        @pl.when(step == tile + 1)
        def _():
            for high in range(2):
                fetch(tile, high).wait()
            if tile + SLOTS - 1 < 4 * tiles:
                for high in range(2):
                    fetch(tile + SLOTS - 1, high).start()

    @pl.when(step > 0)
    def _():
        tile = step - 1
        out[...] = jnp.zeros(out.shape, jnp.bfloat16)
        slot = lax.rem(tile, SLOTS)
        lower = held[slot, 0].reshape(depth // 2, COL_TILE)
        upper = held[slot, 1].reshape(depth // 2, COL_TILE)
        blocks = place.shape[0]
        block_rows = rows // blocks
        for part in range(rows // ROW_TILE):
            span = slice(part * ROW_TILE, (part + 1) * ROW_TILE)
            product = jnp.dot(
                att[span, : depth // 2], lower, preferred_element_type=jnp.float32
            ) + jnp.dot(
                att[span, depth // 2 :], upper, preferred_element_type=jnp.float32
            )
            encoded = (residual[span, :].astype(jnp.float32) + product).astype(jnp.bfloat16)
            for i in range(ROW_TILE // block_rows):
                to = place[part * (ROW_TILE // block_rows) + i] * block_rows
                to = pl.multiple_of(to, block_rows)
                out[pl.ds(to, block_rows), :] = encoded[i * block_rows : (i + 1) * block_rows]


def finish(meta, place, query, pieces, attended, weights, residual):
    rows, width = residual.shape
    depth = weights.shape[0]
    tiles = width // 4 // COL_TILE
    part = weights.shape[0] // 32
    weights = weights.reshape(4, 4, 2, part, width)

    def fixed(s, meta, place):
        return (0, 0)

    def column(s, meta, place):
        tile = jnp.maximum(s - 1, 0)
        low, t, core = tile // (2 * tiles), lax.rem(tile // 2, tiles), lax.rem(tile, 2)
        return (0, (low * 2 + core) * tiles + t)

    steps = 4 * tiles
    return pl.pallas_call(
        finish_kernel,
        grid_spec=pltpu.PrefetchScalarGridSpec(
            num_scalar_prefetch=2,
            grid=(steps + 1,),
            in_specs=[pl.BlockSpec(query.shape, fixed)]
            + [pl.BlockSpec(piece.shape, fixed) for piece in (*pieces, *attended)]
            + [
                pl.BlockSpec(memory_space=pl.ANY),
                pl.BlockSpec((rows, COL_TILE), column),
            ],
            out_specs=pl.BlockSpec((CAP * rows, COL_TILE), column),
            scratch_shapes=[
                pltpu.VMEM((rows, depth), jnp.bfloat16),
                pltpu.VMEM((SLOTS, 2, 4, 4, part, COL_TILE), jnp.bfloat16),
                pltpu.SemaphoreType.DMA((SLOTS, 2)),
            ],
        ),
        out_shape=jax.ShapeDtypeStruct((CAP * rows, width), jnp.bfloat16),
        compiler_params=pltpu.CompilerParams(vmem_limit_bytes=28 * MIB),
        cost_estimate=pl.CostEstimate(
            flops=2 * rows * depth * width,
            bytes_accessed=2 * depth * width + 6 * rows * width,
            transcendentals=0,
        ),
    )(meta, place, query, *pieces, *attended, weights, residual)


def hand_over_kernel(arrived, out, sem):
    copy = pltpu.make_async_copy(arrived, out, sem)
    copy.start()
    copy.wait()


def hand_over(arrived):
    return pl.pallas_call(
        hand_over_kernel,
        in_specs=[pl.BlockSpec(memory_space=pltpu.VMEM)],
        out_specs=pl.BlockSpec(memory_space=pl.ANY),
        out_shape=jax.ShapeDtypeStruct(arrived.shape, arrived.dtype),
        scratch_shapes=[pltpu.SemaphoreType.DMA],
        compiler_params=pltpu.CompilerParams(vmem_limit_bytes=12 * MIB),
    )(arrived)


def shards(queries, keys, values, residual_in, out_weight, lengths, routes):
    req, ctx = lax.axis_index("req"), lax.axis_index("ctx")
    low = ctx // 2
    high = lax.rem(req // 4, 2)
    rows = queries.shape[0]
    req_count = lax.axis_size("req")

    packed = []
    first = 0
    for heads in CHUNKS:
        span = slice(first * HEAD_DIM, (first + heads) * HEAD_DIM)
        packed.append(jnp.concatenate([keys[:, span], values[:, span]], axis=1))
        first += heads

    def ordered(bit, mine, other):
        return jnp.where(
            bit == 0,
            jnp.concatenate([mine, other], axis=1),
            jnp.concatenate([other, mine], axis=1),
        )

    pair = ordered(low, out_weight, flip(out_weight, 0, 2))
    aslant = flip(pair, 4, 2)
    nearest = flip(packed[0], 0, 2)
    nearest, pair, aslant, *packed = lax.optimization_barrier(
        (nearest, pair, aslant, *packed)
    )
    pair = ordered(high, pair, aslant)
    planes = [
        [(y * 8 + h * 4 + x) * 4 + z * 2 + k for y in range(4) for x in range(4) for k in range(2)]
        for h in range(2)
        for z in range(2)
    ]
    weights = lax.all_gather(
        pair, ("req", "ctx"), axis=0, tiled=True, axis_index_groups=planes
    )

    beside = (flip(keys, 0, 1), flip(values, 0, 1))
    positions = jnp.stack([(ctx ^ i) * rows for i in range(4)]).astype(jnp.int32)
    meta = jnp.concatenate([lengths, positions])
    attended = ()
    first = 0
    for i, heads in enumerate(CHUNKS):
        far = flip(packed[i], 0, 2) if i else nearest
        if attended:
            far, *attended = lax.optimization_barrier((far, *attended))
        if i == len(CHUNKS) - 2:
            far, weights = lax.optimization_barrier((far, weights))
        far_beside = flip(far, 0, 1)
        if i == len(CHUNKS) - 1:
            break
        done = attend(meta, queries, (keys, values), beside, far, far_beside, first, heads)
        attended = (*attended, done)
        first += heads

    target = routes[:, 0]
    blocks = target.shape[0]
    order = jnp.arange(blocks, dtype=jnp.int32)
    same = (target[:, None] == target[None, :]) & (order[None, :] < order[:, None])
    cell = target * CAP + jnp.sum(same.astype(jnp.int32), axis=1)

    placed = finish(
        meta,
        cell,
        queries[:, first * HEAD_DIM :],
        (packed[-1], flip(packed[-1], 0, 1), far, far_beside),
        attended,
        weights,
        residual_in,
    )
    width = placed.shape[1]
    arrived = lax.all_to_all(
        placed.reshape(req_count, -1, width), "req", split_axis=0, concat_axis=0, tiled=True
    )
    return hand_over(arrived.reshape(-1, width))


def solution(mesh):
    return jax.shard_map(
        shards,
        mesh=mesh,
        in_specs=(
            P(("req", "ctx"), None),
            P(("req", "ctx"), None),
            P(("req", "ctx"), None),
            P(("req", "ctx"), None),
            P("req", "ctx"),
            P("req"),
            P(("req", "ctx"), None),
        ),
        out_specs=P(("req", "ctx"), None),
        check_vma=False,
    )
```

time: 275 us -> 251 us (0.913)
  waiting for transfers between devices: 77.8 us -> 62.2 us
  local copies, waits for them, and re-layouts: 17 us -> 11.2 us
  Pallas kernels: 43.1 us -> 40.2 us
  other arithmetic: 4.03 us -> 6.8 us
    ppermute x10 -> x13, waiting for transfers between devices: 77.8 us -> 62.2 us  [flip(): return lax.ppermute(x, ('req', 'ctx'), pairs)]
    unnamed x17 -> x20, local copies, waits for them, and re-layouts: 14.1 us -> 6.52 us
    concatenate x3 -> x4, other arithmetic: 2.86 us -> 5.55 us  [shards(): packed.append(jnp.concatenate([keys[:, span], values[:, span]], axis=1))]
    ppermute x10 -> x13, starting transfers between devices: 9.59 us -> 8.47 us  [flip(): return lax.ppermute(x, ('req', 'ctx'), pairs)]
    pallas_call x1 -> x2, Pallas kernels: 19.4 us -> 18.5 us  [the longest x1 15.1 us: finish(): pl.pallas_call(finish_kernel, grid_spec=pltpu.PrefetchScalarGridSpec(num_...]
  transfers between devices with their start and end apart: 11 -> 14, of which waited for: 8 -> 9; matrix products, arithmetic and copies ran while one was open for 1% -> 4% of each run, Pallas kernels for 9% -> 9%
where the time goes in v2:
time: 251 us
  blocking collectives  108 us (43%)
  waiting for transfers between devices  62.2 us (25%)
  Pallas kernels  40.2 us (16%)
  between operations  14.2 us (6%)
  local copies, waits for them, and re-layouts  11.2 us (4%)
  starting transfers between devices  8.47 us (3%)
  other arithmetic  6.8 us (3%)
    all_to_all x1, blocking collectives, shards(): lax.all_to_all(placed.reshape(req_count, -1, width), 'req', split_axis=0,...  108 us
    ppermute x13, waiting for transfers between devices, flip(): return lax.ppermute(x, ('req', 'ctx'), pairs)  62.2 us
    pallas_call x3, Pallas kernels, attend(): pl.pallas_call(attend_kernel, grid_spec=pltpu.PrefetchScalarGridSpec(num_...  21.6 us
    pallas_call x1, Pallas kernels, finish(): pl.pallas_call(finish_kernel, grid_spec=pltpu.PrefetchScalarGridSpec(num_...  15.1 us
    ppermute x13, starting transfers between devices, flip(): return lax.ppermute(x, ('req', 'ctx'), pairs)  8.47 us
    unnamed x20, local copies, waits for them, and re-layouts  6.52 us
    concatenate x4, other arithmetic, shards(): packed.append(jnp.concatenate([keys[:, span], values[:, span]], axis=1))  5.55 us
  transfers between devices with their start and end apart: 14, of which 9 were waited for; matrix products, arithmetic and copies ran while one was open for 4% of the time, Pallas kernels for 9%

profile of v2, /device:TPU:2, one launch (start us, length us, event | category | flops | bytes accessed | tf_op | source)
XLA Modules:
  0.0 251.1 jit_solution(2844866179408451158)
XLA Ops:
  6.5 0.0 all-gather.2.cloned.1.call-start
  6.5 1.9 collective-permute-start.1
  8.5 1.1 fusion.1
  9.5 0.0 slice-start
  9.5 0.0 slice-start.2
  9.6 1.2 fusion.2
  10.7 0.9 pad_maximum_fusion.2
  11.6 0.1 collective-permute-start
  11.7 0.0 slice-done
  11.7 0.0 slice-done.2
  11.7 1.1 pad_maximum_fusion.1
  12.8 0.8 pad_maximum_fusion.3.near
  13.6 0.0 copy-start.8
  13.6 0.0 slice-start.1
  13.7 2.4 slice.30
  16.0 0.0 collective-permute-done.1
  16.0 0.0 copy-done.8
  16.0 0.1 maximum_select_fusion.1
  16.1 0.0 copy-start
  16.1 4.1 %collective-permute-start.2 = (bf16[64,2048]{1,0:T(8,128)(2,1)S(1)}, bf16[64,2048]{1,0:T(8,128)(2,1)S(1)}, u32[]{:S(2)}, u32[]{:S(2)}) collective-permute-start(bf16[64,2048]{1,0:T(8,128)(2,1)S(1)} %maximum_select_fusion.1), channel_id=1, source_target_pairs={{0,18},{1,19},{2,16},{3,17},{4,22},{5,23},{6,20},{7,21},{8,26},{9,... | collective-permute-start | bytes 786440 | tf_op jit(solution)/shard_map/ppermute | solution.py:28
  20.2 0.0 slice-done.1
  20.2 2.7 %pad_maximum_fusion = bf16[512,2048]{1,0:T(8,128)(2,1)} fusion(bf16[512,1024]{1,0:T(8,128)(2,1)S(1)} %slice-done.1, bf16[512,1024]{1,0:T(8,128)(2,1)} %slice.30), kind=kLoop, calls=%fused_computation | loop fusion | flops 4194304 | bytes 4194304 | tf_op jit(solution)/shard_map/concatenate | solution.py:242
  23.0 3.0 %collective-permute-done.2 = bf16[64,2048]{1,0:T(8,128)(2,1)S(1)} collective-permute-done((bf16[64,2048]{1,0:T(8,128)(2,1)S(1)}, bf16[64,2048]{1,0:T(8,128)(2,1)S(1)}, u32[]{:S(2)}, u32[]{:S(2)}) %collective-permute-start.2) | collective-permute-done | bytes 262176 | tf_op jit(solution)/shard_map/ppermute | solution.py:28
  26.0 0.0 collective-permute-done.k2.v2
  26.0 1.0 maximum_select_fusion
  27.0 0.0 all-gather.2.cloned.1.call-update
  27.0 0.1 collective-permute-start.7
  27.1 0.0 copy-done
  27.1 0.5 collective-permute-start.8
  27.6 0.0 collective-permute-start.6
  27.6 0.1 collective-permute-start.9
  28.4 0.1 concatenate.27.meta
  28.4 6.4 %collective-permute-done.9.k3.v3 = bf16[512,512]{1,0:T(8,128)(2,1)S(1)} collective-permute-done((bf16[512,512]{1,0:T(8,128)(2,1)}, bf16[512,512]{1,0:T(8,128)(2,1)S(1)}, u32[]{:S(2)}, u32[]{:S(2)}) %collective-permute-start.9) | collective-permute-done | bytes 524320 | tf_op jit(solution)/shard_map/ppermute | solution.py:28
  34.9 0.0 collective-permute-done.7.k1
  34.9 0.2 collective-permute-done.8.v1
  35.1 0.0 copy-start.1
  35.1 1.6 copy-done.1
  36.7 1.7 copy-done.3
  38.4 4.0 %shard_map.73.refs_0_ = bf16[512,256]{1,0:T(8,128)(2,1)S(1)} custom-call(s32[5]{0:T(128)S(1)} %concatenate.27.meta, bf16[512,2048]{1,0:T(8,128)(2,1)S(1)} %copy-done.3, bf16[512,2048]{1,0:T(8,128)(2,1)S(1)} %copy-done.1, bf16[512,2048]{1,0:T(8,128)(2,1)S(1)} %copy-done, bf16[512,2048]{1,0:T(8,128)(2,1)} %collective-permute-done.7.k1, ...), custom_call_target="tpu_custom_call" | custom-call | tf_op jit(solution)/shard_map/pallas_call | solution.py:84
  42.5 33.1 %collective-permute-done.6.k2.v2 = bf16[512,2048]{1,0:T(8,128)(2,1)} collective-permute-done((bf16[512,2048]{1,0:T(8,128)(2,1)}, bf16[512,2048]{1,0:T(8,128)(2,1)}, u32[]{:S(2)}, u32[]{:S(2)}) %collective-permute-start.6) | collective-permute-done | bytes 2097184 | tf_op jit(solution)/shard_map/ppermute | solution.py:28
  75.6 0.0 collective-permute-start.10
  75.6 0.0 copy-done.7
  75.6 0.3 collective-permute-start.5
  75.8 4.3 %collective-permute-done.10.k3.v3 = bf16[512,2048]{1,0:T(8,128)(2,1)S(1)} collective-permute-done((bf16[512,2048]{1,0:T(8,128)(2,1)}, bf16[512,2048]{1,0:T(8,128)(2,1)S(1)}, u32[]{:S(2)}, u32[]{:S(2)}) %collective-permute-start.10) | collective-permute-done | bytes 2097184 | tf_op jit(solution)/shard_map/ppermute | solution.py:28
  80.2 11.0 %shard_map.74.refs_1_ = bf16[512,1024]{1,0:T(8,128)(2,1)S(1)} custom-call(s32[5]{0:T(128)S(1)} %concatenate.27.meta, bf16[512,2048]{1,0:T(8,128)(2,1)S(1)} %copy-done.3, bf16[512,2048]{1,0:T(8,128)(2,1)S(1)} %copy-done.1, bf16[512,2048]{1,0:T(8,128)(2,1)S(1)} %copy-done, bf16[512,2048]{1,0:T(8,128)(2,1)} %collective-permute-done.7.k1, ...), custom_call_target="tpu_custom_call" | custom-call | tf_op jit(solution)/shard_map/pallas_call | solution.py:84
  91.2 10.0 %collective-permute-done.5.k2.v2 = bf16[512,1024]{1,0:T(8,128)(2,1)} collective-permute-done((bf16[512,1024]{1,0:T(8,128)(2,1)S(1)}, bf16[512,1024]{1,0:T(8,128)(2,1)}, u32[]{:S(2)}, u32[]{:S(2)}) %collective-permute-start.5) | collective-permute-done | bytes 1048608 | tf_op jit(solution)/shard_map/ppermute | solution.py:28
  101.2 0.0 collective-permute-start.11
  101.2 1.4 collective-permute-start.4
  102.6 0.0 collective-permute-start.3
  102.6 1.5 collective-permute-done.11.k3.v3
  104.1 1.6 copy-done.2
  105.7 1.6 copy-done.4
  107.3 6.6 %shard_map.75.refs_2_ = bf16[512,512]{1,0:T(8,128)(2,1)S(1)} custom-call(s32[5]{0:T(128)S(1)} %concatenate.27.meta, bf16[512,2048]{1,0:T(8,128)(2,1)S(1)} %copy-done.4, bf16[512,2048]{1,0:T(8,128)(2,1)S(1)} %copy-done.2, bf16[512,2048]{1,0:T(8,128)(2,1)S(1)} %copy-done, bf16[512,2048]{1,0:T(8,128)(2,1)} %collective-permute-done.7.k1, ...), custom_call_target="tpu_custom_call" | custom-call | tf_op jit(solution)/shard_map/pallas_call | solution.py:84
  113.9 1.9 collective-permute-done.4.far
  115.8 0.0 collective-permute-start.12
  115.8 0.0 copy-done.9
  115.8 0.2 convert_reduce_fusion
  116.0 0.0 collective-permute-done.3.near_beside
  116.0 1.7 collective-permute-done.12.far_beside
  117.7 0.0 copy-done.5
  117.7 0.0 copy-done.6
  117.7 15.1 %shard_map.76 = bf16[1024,4096]{1,0:T(8,128)(2,1)S(1)} custom-call(s32[5]{0:T(128)S(1)} %concatenate.27.meta, s32[32]{0:T(128)S(1)} %multiply_add_fusion.place, bf16[512,256]{1,0:T(8,128)(2,1)S(1)} %slice.27.q, bf16[512,512]{1,0:T(8,128)(2,1)S(1)} %copy-done.6, bf16[512,512]{1,0:T(8,128)(2,1)S(1)} %collective-permute-done.3.near_beside, ...), custom_call_target="tpu_custom_call" | custom-call | flops 8589934592 | bytes 29360128 | tf_op jit(solution)/shard_map/pallas_call | solution.py:186
  132.9 108.0 %all_to_all.5 = bf16[32,32,4096]{2,1,0:T(8,128)(2,1)S(1)} all-to-all(bf16[32,32,4096]{2,1,0:T(8,128)(2,1)S(1)} %bitcast.9), channel_id=1, replica_groups=mesh['req'=32,'ctx'=4] {'req'}, dimensions={0} | all-to-all | bytes 16777216 | tf_op jit(solution)/shard_map/all_to_all | solution.py:302
  240.9 3.4 %shard_map.77 = bf16[1024,4096]{1,0:T(8,128)(2,1)} custom-call(bf16[1024,4096]{1,0:T(8,128)(2,1)S(1)} %bitcast.10), custom_call_target="tpu_custom_call" | custom-call | tf_op jit(solution)/shard_map/pallas_call | solution.py:221
  (10 shorter events, 0.1 us)
Async XLA Ops:
  6.5 94.7 %all-gather.2.cloned.1.call-start = ((), (), s32[]{:S(2)}) async-start(), calls=%async_computation.1 | async-start | bytes 17301504 | tf_op jit(solution)/shard_map/all_gather | solution.py:264
  6.5 9.5 %collective-permute-start.1 = (bf16[64,1024]{1,0:T(8,128)(2,1)}, bf16[64,1024]{1,0:T(8,128)(2,1)S(1)}, u32[]{:S(2)}, u32[]{:S(2)}) collective-permute-start(bf16[64,1024]{1,0:T(8,128)(2,1)} %param.11), channel_id=1, source_target_pairs={{0,2},{1,3},{2,0},{3,1},{4,6},{5,7},{6,4},{7,5},{8,10},{9,11},{10,... | collective-permute-start | bytes 393224 | tf_op jit(solution)/shard_map/ppermute | solution.py:28
  9.5 2.1 slice-start
  9.5 2.1 slice-start.2
  11.6 14.4 %collective-permute-start = (bf16[512,512]{1,0:T(8,128)(2,1)}, bf16[512,512]{1,0:T(8,128)(2,1)}, u32[]{:S(2)}, u32[]{:S(2)}) collective-permute-start(bf16[512,512]{1,0:T(8,128)(2,1)} %pad_maximum_fusion.2), channel_id=1, source_target_pairs={{0,2},{1,3},{2,0},{3,1},{4,6},{5,7},{6,4},{7,5},{8,10},{9,11},{10,... | collective-permute-start | bytes 1572872 | tf_op jit(solution)/shard_map/ppermute | solution.py:28
  13.6 2.4 copy-start.8
  13.6 6.6 %slice-start.1 = ((bf16[512,2048]{1,0:T(8,128)(2,1)}), bf16[512,1024]{1,0:T(8,128)(2,1)S(1)}, s32[]{:S(2)}) async-start(bf16[512,2048]{1,0:T(8,128)(2,1)} %v0.5), calls=%async_computation.3 | async-start | bytes 2097152 | tf_op jit(solution)/shard_map/slice | solution.py:242
  16.1 11.0 %copy-start = (bf16[512,2048]{1,0:T(8,128)(2,1)S(1)}, bf16[512,2048]{1,0:T(8,128)(2,1)}, u32[]{:S(2)}) copy-start(bf16[512,2048]{1,0:T(8,128)(2,1)} %v0.5) | copy-start | bytes 6291460
  16.1 9.9 %collective-permute-start.2 = (bf16[64,2048]{1,0:T(8,128)(2,1)S(1)}, bf16[64,2048]{1,0:T(8,128)(2,1)S(1)}, u32[]{:S(2)}, u32[]{:S(2)}) collective-permute-start(bf16[64,2048]{1,0:T(8,128)(2,1)S(1)} %maximum_select_fusion.1), channel_id=1, source_target_pairs={{0,18},{1,19},{2,16},{3,17},{4,22},{5,23},{6,20},{7,21},{8,26},{9,... | collective-permute-start | bytes 786440 | tf_op jit(solution)/shard_map/ppermute | solution.py:28
  27.0 7.9 %collective-permute-start.7 = (bf16[512,2048]{1,0:T(8,128)(2,1)}, bf16[512,2048]{1,0:T(8,128)(2,1)}, u32[]{:S(2)}, u32[]{:S(2)}) collective-permute-start(bf16[512,2048]{1,0:T(8,128)(2,1)} %k0.5), channel_id=1, source_target_pairs={{0,1},{1,0},{2,3},{3,2},{4,5},{5,4},{6,7},{7,6},{8,9},{9,8},{10,11... | collective-permute-start | bytes 6291464 | tf_op jit(solution)/shard_map/ppermute | solution.py:28
  27.1 8.0 %collective-permute-start.8 = (bf16[512,2048]{1,0:T(8,128)(2,1)S(1)}, bf16[512,2048]{1,0:T(8,128)(2,1)}, u32[]{:S(2)}, u32[]{:S(2)}) collective-permute-start(bf16[512,2048]{1,0:T(8,128)(2,1)S(1)} %copy-done), channel_id=1, source_target_pairs={{0,1},{1,0},{2,3},{3,2},{4,5},{5,4},{6,7},{7,6},{8,9},{9,8},{10,11... | collective-permute-start | bytes 6291464 | tf_op jit(solution)/shard_map/ppermute | solution.py:28
  27.6 48.0 %collective-permute-start.6 = (bf16[512,2048]{1,0:T(8,128)(2,1)}, bf16[512,2048]{1,0:T(8,128)(2,1)}, u32[]{:S(2)}, u32[]{:S(2)}) collective-permute-start(bf16[512,2048]{1,0:T(8,128)(2,1)} %pad_maximum_fusion), channel_id=1, source_target_pairs={{0,2},{1,3},{2,0},{3,1},{4,6},{5,7},{6,4},{7,5},{8,10},{9,11},{10,... | collective-permute-start | bytes 6291464 | tf_op jit(solution)/shard_map/ppermute | solution.py:28
  27.6 7.3 %collective-permute-start.9 = (bf16[512,512]{1,0:T(8,128)(2,1)}, bf16[512,512]{1,0:T(8,128)(2,1)S(1)}, u32[]{:S(2)}, u32[]{:S(2)}) collective-permute-start(bf16[512,512]{1,0:T(8,128)(2,1)} %collective-permute-done.k2.v2), channel_id=1, source_target_pairs={{0,1},{1,0},{2,3},{3,2},{4,5},{5,4},{6,7},{7,6},{8,9},{9,8},{10,11... | collective-permute-start | bytes 1572872 | tf_op jit(solution)/shard_map/ppermute | solution.py:28
  35.1 1.6 copy-start.1
  36.7 1.7 copy-start.3
  38.4 37.1 %copy-start.7 = (bf16[512,1024]{1,0:T(8,128)(2,1)S(1)}, bf16[512,1024]{1,0:T(8,128)(2,1)}, u32[]{:S(2)}) copy-start(bf16[512,1024]{1,0:T(8,128)(2,1)} %pad_maximum_fusion.1) | copy-start | bytes 3145732
  75.6 4.6 %collective-permute-start.10 = (bf16[512,2048]{1,0:T(8,128)(2,1)}, bf16[512,2048]{1,0:T(8,128)(2,1)S(1)}, u32[]{:S(2)}, u32[]{:S(2)}) collective-permute-start(bf16[512,2048]{1,0:T(8,128)(2,1)} %collective-permute-done.6.k2.v2), channel_id=1, source_target_pairs={{0,1},{1,0},{2,3},{3,2},{4,5},{5,4},{6,7},{7,6},{8,9},{9,8},{10,11... | collective-permute-start | bytes 6291464 | tf_op jit(solution)/shard_map/ppermute | solution.py:28
  75.6 25.7 %collective-permute-start.5 = (bf16[512,1024]{1,0:T(8,128)(2,1)S(1)}, bf16[512,1024]{1,0:T(8,128)(2,1)}, u32[]{:S(2)}, u32[]{:S(2)}) collective-permute-start(bf16[512,1024]{1,0:T(8,128)(2,1)S(1)} %copy-done.7), channel_id=1, source_target_pairs={{0,2},{1,3},{2,0},{3,1},{4,6},{5,7},{6,4},{7,5},{8,10},{9,11},{10,... | collective-permute-start | bytes 3145736 | tf_op jit(solution)/shard_map/ppermute | solution.py:28
  80.2 35.6 %copy-start.9 = (s32[32,1]{0,1:T(1,128)S(1)}, s32[32,1]{0,1:T(1,128)}, u32[]{:S(2)}) copy-start(s32[32,1]{0,1:T(1,128)} %param.13) | copy-start | bytes 388
  101.2 2.9 %collective-permute-start.11 = (bf16[512,1024]{1,0:T(8,128)(2,1)}, bf16[512,1024]{1,0:T(8,128)(2,1)S(1)}, u32[]{:S(2)}, u32[]{:S(2)}) collective-permute-start(bf16[512,1024]{1,0:T(8,128)(2,1)} %collective-permute-done.5.k2.v2), channel_id=1, source_target_pairs={{0,1},{1,0},{2,3},{3,2},{4,5},{5,4},{6,7},{7,6},{8,9},{9,8},{10,11... | collective-permute-start | bytes 3145736 | tf_op jit(solution)/shard_map/ppermute | solution.py:28
  101.2 14.5 %collective-permute-start.4 = (bf16[512,512]{1,0:T(8,128)(2,1)}, bf16[512,512]{1,0:T(8,128)(2,1)S(1)}, u32[]{:S(2)}, u32[]{:S(2)}) collective-permute-start(bf16[512,512]{1,0:T(8,128)(2,1)} %pad_maximum_fusion.3.near), channel_id=1, source_target_pairs={{0,2},{1,3},{2,0},{3,1},{4,6},{5,7},{6,4},{7,5},{8,10},{9,11},{10,... | collective-permute-start | bytes 1572872 | tf_op jit(solution)/shard_map/ppermute | solution.py:28
  102.6 13.4 %collective-permute-start.3 = (bf16[512,512]{1,0:T(8,128)(2,1)}, bf16[512,512]{1,0:T(8,128)(2,1)S(1)}, u32[]{:S(2)}, u32[]{:S(2)}) collective-permute-start(bf16[512,512]{1,0:T(8,128)(2,1)} %pad_maximum_fusion.3.near), channel_id=1, source_target_pairs={{0,1},{1,0},{2,3},{3,2},{4,5},{5,4},{6,7},{7,6},{8,9},{9,8},{10,11... | collective-permute-start | bytes 1572872 | tf_op jit(solution)/shard_map/ppermute | solution.py:28
  104.1 1.6 copy-start.2
  105.7 1.6 copy-start.4
  107.3 10.4 %copy-start.5 = (bf16[512,4096]{1,0:T(8,128)(2,1)S(1)}, bf16[512,4096]{1,0:T(8,128)(2,1)}, u32[]{:S(2)}) copy-start(bf16[512,4096]{1,0:T(8,128)(2,1)} %refs_4_.1) | copy-start | bytes 12582916
  107.3 10.4 %copy-start.6 = (bf16[512,512]{1,0:T(8,128)(2,1)S(1)}, bf16[512,512]{1,0:T(8,128)(2,1)}, u32[]{:S(2)}) copy-start(bf16[512,512]{1,0:T(8,128)(2,1)} %pad_maximum_fusion.3.near) | copy-start | bytes 1572868
  115.8 1.9 collective-permute-start.12
Sparse Core Ops, SparseCore 0:
  27.1 73.6 all-gather.1

commit v3 on v2

--- a/solution.py
+++ b/solution.py
@@ -67,12 +67,9 @@
     attend_head(meta, q, (k0, k1, k2, k3), (v0, v1, v2, v3), out)
 
 
-def attend(meta, queries, own, beside, far, far_beside, first, heads):
-    rows = queries.shape[0]
-    count = own[0].shape[0]
-
-    def whole(g, meta):
-        return (0, first + g)
+def attend(meta, query, pieces):
+    rows, width = query.shape
+    heads = width // HEAD_DIM
 
     def key_of(g, meta):
         return (0, g)
@@ -80,23 +77,21 @@
     def value_of(g, meta):
         return (0, heads + g)
 
-    block = lambda n, index: pl.BlockSpec((n, HEAD_DIM), index)
+    block = lambda index: pl.BlockSpec((rows, HEAD_DIM), index)
     return pl.pallas_call(
         attend_kernel,
         grid_spec=pltpu.PrefetchScalarGridSpec(
             num_scalar_prefetch=1,
             grid=(heads,),
-            in_specs=[block(rows, whole)]
-            + [block(count, whole)] * 4
-            + [block(count, key_of), block(count, value_of)] * 2,
-            out_specs=block(rows, key_of),
-        ),
-        out_shape=jax.ShapeDtypeStruct((rows, heads * HEAD_DIM), jnp.bfloat16),
+            in_specs=[block(key_of)] + [block(key_of), block(value_of)] * 4,
+            out_specs=block(key_of),
+        ),
+        out_shape=jax.ShapeDtypeStruct(query.shape, jnp.bfloat16),
         compiler_params=pltpu.CompilerParams(vmem_limit_bytes=20 * MIB),
         cost_estimate=pl.CostEstimate(
             flops=0, bytes_accessed=0, transcendentals=0
         ),
-    )(meta, queries, *own, *beside, far, far, far_beside, far_beside)
+    )(meta, query, *[piece for piece in pieces for _ in range(2)])
 
 
 def finish_kernel(meta, place, q, near, near_beside, far, far_beside, *refs):
@@ -252,9 +247,7 @@
     pair = ordered(low, out_weight, flip(out_weight, 0, 2))
     aslant = flip(pair, 4, 2)
     nearest = flip(packed[0], 0, 2)
-    nearest, pair, aslant, *packed = lax.optimization_barrier(
-        (nearest, pair, aslant, *packed)
-    )
+    nearest, pair, aslant, *_ = lax.optimization_barrier((nearest, pair, aslant, *packed))
     pair = ordered(high, pair, aslant)
     planes = [
         [(y * 8 + h * 4 + x) * 4 + z * 2 + k for y in range(4) for x in range(4) for k in range(2)]
@@ -265,7 +258,7 @@
         pair, ("req", "ctx"), axis=0, tiled=True, axis_index_groups=planes
     )
 
-    beside = (flip(keys, 0, 1), flip(values, 0, 1))
+    beside = [flip(near, 0, 1) for near in packed]
     positions = jnp.stack([(ctx ^ i) * rows for i in range(4)]).astype(jnp.int32)
     meta = jnp.concatenate([lengths, positions])
     attended = ()
@@ -279,7 +272,8 @@
         far_beside = flip(far, 0, 1)
         if i == len(CHUNKS) - 1:
             break
-        done = attend(meta, queries, (keys, values), beside, far, far_beside, first, heads)
+        query = queries[:, first * HEAD_DIM : (first + heads) * HEAD_DIM]
+        done = attend(meta, query, (packed[i], beside[i], far, far_beside))
         attended = (*attended, done)
         first += heads
 
@@ -293,7 +287,7 @@
         meta,
         cell,
         queries[:, first * HEAD_DIM :],
-        (packed[-1], flip(packed[-1], 0, 1), far, far_beside),
+        (packed[-1], beside[-1], far, far_beside),
         attended,
         weights,
         residual_in,

time: 251 us -> 249 us (level)
    unnamed x20 -> x18, local copies, waits for them, and re-layouts: 6.52 us -> 1.01 us
    slice x1 -> x3, local copies, waits for them, and re-layouts: 0.03 us -> 2.94 us  [shards(): query = queries[:, first * HEAD_DIM:(first + heads) * HEAD_DIM]]
    ppermute x13 -> x14, starting transfers between devices: 8.47 us -> 9.55 us  [flip(): return lax.ppermute(x, ('req', 'ctx'), pairs)]
    slice x9 -> x7, local copies, waits for them, and re-layouts: 4.61 us -> 5.07 us  [shards(): packed.append(jnp.concatenate([keys[:, span], values[:, span]], axis=1))]
    ppermute x13 -> x14, waiting for transfers between devices: 62.2 us -> 62 us  [flip(): return lax.ppermute(x, ('req', 'ctx'), pairs)]
  transfers between devices with their start and end apart: 14 -> 15, of which waited for: 9 -> 8; matrix products, arithmetic and copies ran while one was open for 4% -> 5% of each run, Pallas kernels for 9% -> 9%
where the time goes in v3:
time: 249 us; the launch traced here: 248 us
  blocking collectives  107 us (43%)
  waiting for transfers between devices  63.7 us (26%)
  Pallas kernels  40.3 us (16%)
  between operations  14.3 us (6%)
  starting transfers between devices  9.55 us (4%)
  local copies, waits for them, and re-layouts  9.1 us (4%)
  other arithmetic  4.72 us (2%)
    all_to_all x1, blocking collectives, shards(): lax.all_to_all(placed.reshape(req_count, -1, width), 'req', split_axis=0,...  107 us
    ppermute x14, waiting for transfers between devices, flip(): return lax.ppermute(x, ('req', 'ctx'), pairs)  62 us
    pallas_call x3, Pallas kernels, attend(): pl.pallas_call(attend_kernel, grid_spec=pltpu.PrefetchScalarGridSpec(num_...  21.8 us
    pallas_call x1, Pallas kernels, finish(): pl.pallas_call(finish_kernel, grid_spec=pltpu.PrefetchScalarGridSpec(num_...  15.1 us
    ppermute x14, starting transfers between devices, flip(): return lax.ppermute(x, ('req', 'ctx'), pairs)  9.55 us
    slice x7, local copies, waits for them, and re-layouts, shards(): packed.append(jnp.concatenate([keys[:, span], values[:, span]], axis=1))  5.07 us
  transfers between devices with their start and end apart: 15, of which 8 were waited for; matrix products, arithmetic and copies ran while one was open for 5% of the time, Pallas kernels for 9%

profile of v3, /device:TPU:2, one launch (start us, length us, event | category | flops | bytes accessed | tf_op | source)
XLA Modules:
  0.0 248.2 jit_solution(8109729910752736999)
XLA Ops:
  6.5 0.0 all-gather.2.cloned.1.call-start
  6.5 1.9 collective-permute-start.6
  8.5 1.3 fusion.1
  9.7 0.0 slice-start
  9.7 0.0 slice-start.1
  9.8 0.9 pad_maximum_fusion.3.k0.v0
  10.6 0.1 collective-permute-start.5
  10.7 0.2 slice-done
  11.0 0.2 slice-done.1
  11.1 0.1 pad_maximum_fusion.1.k0.v0
  11.3 0.0 copy-start.5
  11.3 0.9 pad_maximum_fusion.2.near
  12.1 2.3 slice.41
  14.5 0.0 copy-done.5
  14.5 1.1 slice.42
  15.5 0.0 collective-permute-done.6
  15.5 0.1 maximum_select_fusion.1
  15.6 3.7 %collective-permute-start.7 = (bf16[64,2048]{1,0:T(8,128)(2,1)S(1)}, bf16[64,2048]{1,0:T(8,128)(2,1)S(1)}, u32[]{:S(2)}, u32[]{:S(2)}) collective-permute-start(bf16[64,2048]{1,0:T(8,128)(2,1)S(1)} %maximum_select_fusion.1), channel_id=1, source_target_pairs={{0,18},{1,19},{2,16},{3,17},{4,22},{5,23},{6,20},{7,21},{8,26},{9,... | collective-permute-start | bytes 786440 | tf_op jit(solution)/shard_map/ppermute | solution.py:28
  19.3 1.7 pad_maximum_fusion.k0.v0
  21.0 4.0 %collective-permute-done.7 = bf16[64,2048]{1,0:T(8,128)(2,1)S(1)} collective-permute-done((bf16[64,2048]{1,0:T(8,128)(2,1)S(1)}, bf16[64,2048]{1,0:T(8,128)(2,1)S(1)}, u32[]{:S(2)}, u32[]{:S(2)}) %collective-permute-start.7) | collective-permute-done | bytes 262176 | tf_op jit(solution)/shard_map/ppermute | solution.py:28
  25.1 0.0 collective-permute-done.5.k2.v2
  25.1 0.9 maximum_select_fusion
  26.0 0.0 all-gather.2.cloned.1.call-update
  26.0 0.3 collective-permute-start.3
  26.3 0.0 collective-permute-start.4
  26.3 0.5 collective-permute-start.8
  26.8 0.0 collective-permute-start.9
  27.5 0.1 concatenate.27.meta
  27.5 1.8 fusion.3
  29.3 0.0 collective-permute-done.4.k1.v1
  29.3 0.7 collective-permute-done.8.k3.v3
  30.0 4.3 %shard_map.73.refs_0_ = bf16[512,256]{1,0:T(8,128)(2,1)S(1)} custom-call(s32[5]{0:T(128)S(1)} %concatenate.27.meta, bf16[512,256]{1,0:T(8,128)(2,1)S(1)} %get-tuple-element.37.q, bf16[512,512]{1,0:T(8,128)(2,1)} %pad_maximum_fusion.3.k0.v0, bf16[512,512]{1,0:T(8,128)(2,1)} %pad_maximum_fusion.3.k0.v0, bf16[512,512]{1,0:T(8,128)(2,1)} %collective-permute-done.4.k1.v1, ...), custom_call_target="tpu_custom_call" | custom-call | tf_op jit(solution)/shard_map/pallas_call | solution.py:81
  34.3 38.1 %collective-permute-done.3.k2.v2 = bf16[512,2048]{1,0:T(8,128)(2,1)} collective-permute-done((bf16[512,2048]{1,0:T(8,128)(2,1)S(1)}, bf16[512,2048]{1,0:T(8,128)(2,1)}, u32[]{:S(2)}, u32[]{:S(2)}) %collective-permute-start.3) | collective-permute-done | bytes 2097184 | tf_op jit(solution)/shard_map/ppermute | solution.py:28
  72.4 0.0 collective-permute-start.10
  72.4 1.0 collective-permute-start.2
  73.4 0.2 collective-permute-start.11
  73.6 0.1 slice.46.q
  73.7 0.0 collective-permute-done.9.k1.v1
  73.7 3.4 %collective-permute-done.10.k3.v3 = bf16[512,2048]{1,0:T(8,128)(2,1)S(1)} collective-permute-done((bf16[512,2048]{1,0:T(8,128)(2,1)}, bf16[512,2048]{1,0:T(8,128)(2,1)S(1)}, u32[]{:S(2)}, u32[]{:S(2)}) %collective-permute-start.10) | collective-permute-done | bytes 2097184 | tf_op jit(solution)/shard_map/ppermute | solution.py:28
  77.2 11.0 %shard_map.74.refs_1_ = bf16[512,1024]{1,0:T(8,128)(2,1)S(1)} custom-call(s32[5]{0:T(128)S(1)} %concatenate.27.meta, bf16[512,1024]{1,0:T(8,128)(2,1)S(1)} %slice.46.q, bf16[512,2048]{1,0:T(8,128)(2,1)S(1)} %pad_maximum_fusion.k0.v0, bf16[512,2048]{1,0:T(8,128)(2,1)S(1)} %pad_maximum_fusion.k0.v0, bf16[512,2048]{1,0:T(8,128)(2,1)} %collective-permute-done.9.k1.v1, ...), custom_call_target="tpu_custom_call" | custom-call | tf_op jit(solution)/shard_map/pallas_call | solution.py:81
  88.2 0.0 copy-start.1
  88.2 1.0 copy-done.1
  89.1 8.9 %collective-permute-done.2.k2.v2 = bf16[512,1024]{1,0:T(8,128)(2,1)} collective-permute-done((bf16[512,1024]{1,0:T(8,128)(2,1)S(1)}, bf16[512,1024]{1,0:T(8,128)(2,1)}, u32[]{:S(2)}, u32[]{:S(2)}) %collective-permute-start.2) | collective-permute-done | bytes 1048608 | tf_op jit(solution)/shard_map/ppermute | solution.py:28
  98.1 1.7 all-gather.2.cloned.1.call-done
  99.8 0.3 collective-permute-start.12
  100.1 1.6 collective-permute-start.1
  101.6 0.0 collective-permute-start
  101.6 1.1 slice.47.q
  102.7 0.0 copy-start.8
  102.7 0.0 copy-start
  102.7 0.0 copy-start.2
  102.7 0.0 collective-permute-done.11.k1.v1
  102.8 0.0 collective-permute-done.12.k3.v3
  102.8 6.6 %shard_map.75.refs_2_ = bf16[512,512]{1,0:T(8,128)(2,1)S(1)} custom-call(s32[5]{0:T(128)S(1)} %concatenate.27.meta, bf16[512,512]{1,0:T(8,128)(2,1)S(1)} %slice.47.q, bf16[512,1024]{1,0:T(8,128)(2,1)S(1)} %pad_maximum_fusion.1.k0.v0, bf16[512,1024]{1,0:T(8,128)(2,1)S(1)} %pad_maximum_fusion.1.k0.v0, bf16[512,1024]{1,0:T(8,128)(2,1)} %collective-permute-done.11.k1.v1, ...), custom_call_target="tpu_custom_call" | custom-call | tf_op jit(solution)/shard_map/pallas_call | solution.py:81
  109.3 5.0 %collective-permute-done.1.far = bf16[512,512]{1,0:T(8,128)(2,1)S(1)} collective-permute-done((bf16[512,512]{1,0:T(8,128)(2,1)}, bf16[512,512]{1,0:T(8,128)(2,1)S(1)}, u32[]{:S(2)}, u32[]{:S(2)}) %collective-permute-start.1) | collective-permute-done | bytes 524320 | tf_op jit(solution)/shard_map/ppermute | solution.py:28
  114.3 0.0 collective-permute-start.13
  114.3 0.0 copy-done.8
  114.4 0.2 convert_reduce_fusion
  114.5 0.0 collective-permute-done.near_beside
  114.5 1.7 collective-permute-done.13.far_beside
  116.3 0.0 copy-done.4
  116.3 15.1 %shard_map.76 = bf16[1024,4096]{1,0:T(8,128)(2,1)S(1)} custom-call(s32[5]{0:T(128)S(1)} %concatenate.27.meta, s32[32]{0:T(128)S(1)} %multiply_add_fusion.place, bf16[512,256]{1,0:T(8,128)(2,1)S(1)} %copy-done.4, bf16[512,512]{1,0:T(8,128)(2,1)S(1)} %copy-done.3, bf16[512,512]{1,0:T(8,128)(2,1)S(1)} %collective-permute-done.near_beside, ...), custom_call_target="tpu_custom_call" | custom-call | flops 8589934592 | bytes 29360128 | tf_op jit(solution)/shard_map/pallas_call | solution.py:181
  131.4 106.5 %all_to_all.5 = bf16[32,32,4096]{2,1,0:T(8,128)(2,1)S(1)} all-to-all(bf16[32,32,4096]{2,1,0:T(8,128)(2,1)S(1)} %bitcast.9), channel_id=1, replica_groups=mesh['req'=32,'ctx'=4] {'req'}, dimensions={0} | all-to-all | bytes 16777216 | tf_op jit(solution)/shard_map/all_to_all | solution.py:296
  237.9 3.4 %shard_map.77 = bf16[1024,4096]{1,0:T(8,128)(2,1)} custom-call(bf16[1024,4096]{1,0:T(8,128)(2,1)S(1)} %bitcast.10), custom_call_target="tpu_custom_call" | custom-call | tf_op jit(solution)/shard_map/pallas_call | solution.py:216
  (10 shorter events, 0.0 us)
Async XLA Ops:
  6.5 93.3 %all-gather.2.cloned.1.call-start = ((), (), s32[]{:S(2)}) async-start(), calls=%async_computation.1 | async-start | bytes 17301504 | tf_op jit(solution)/shard_map/all_gather | solution.py:257
  6.5 9.0 %collective-permute-start.6 = (bf16[64,1024]{1,0:T(8,128)(2,1)}, bf16[64,1024]{1,0:T(8,128)(2,1)S(1)}, u32[]{:S(2)}, u32[]{:S(2)}) collective-permute-start(bf16[64,1024]{1,0:T(8,128)(2,1)} %param.11), channel_id=1, source_target_pairs={{0,2},{1,3},{2,0},{3,1},{4,6},{5,7},{6,4},{7,5},{8,10},{9,11},{10,... | collective-permute-start | bytes 393224 | tf_op jit(solution)/shard_map/ppermute | solution.py:28
  9.7 1.2 slice-start
  9.7 1.4 slice-start.1
  10.6 14.5 %collective-permute-start.5 = (bf16[512,512]{1,0:T(8,128)(2,1)}, bf16[512,512]{1,0:T(8,128)(2,1)}, u32[]{:S(2)}, u32[]{:S(2)}) collective-permute-start(bf16[512,512]{1,0:T(8,128)(2,1)} %pad_maximum_fusion.3.k0.v0), channel_id=1, source_target_pairs={{0,2},{1,3},{2,0},{3,1},{4,6},{5,7},{6,4},{7,5},{8,10},{9,11},{10,... | collective-permute-start | bytes 1572872 | tf_op jit(solution)/shard_map/ppermute | solution.py:28
  11.3 3.2 %copy-start.5 = (bf16[512,2048]{1,0:T(8,128)(2,1)S(1)}, bf16[512,2048]{1,0:T(8,128)(2,1)}, u32[]{:S(2)}) copy-start(bf16[512,2048]{1,0:T(8,128)(2,1)} %param.9) | copy-start | bytes 6291460
  12.1 3.4 %copy-start.7 = (bf16[64,1024]{1,0:T(8,128)(2,1)S(1)}, bf16[64,1024]{1,0:T(8,128)(2,1)}, u32[]{:S(2)}) copy-start(bf16[64,1024]{1,0:T(8,128)(2,1)} %param.11) | copy-start | bytes 393220
  15.6 9.5 %collective-permute-start.7 = (bf16[64,2048]{1,0:T(8,128)(2,1)S(1)}, bf16[64,2048]{1,0:T(8,128)(2,1)S(1)}, u32[]{:S(2)}, u32[]{:S(2)}) collective-permute-start(bf16[64,2048]{1,0:T(8,128)(2,1)S(1)} %maximum_select_fusion.1), channel_id=1, source_target_pairs={{0,18},{1,19},{2,16},{3,17},{4,22},{5,23},{6,20},{7,21},{8,26},{9,... | collective-permute-start | bytes 786440 | tf_op jit(solution)/shard_map/ppermute | solution.py:28
  26.0 46.4 %collective-permute-start.3 = (bf16[512,2048]{1,0:T(8,128)(2,1)S(1)}, bf16[512,2048]{1,0:T(8,128)(2,1)}, u32[]{:S(2)}, u32[]{:S(2)}) collective-permute-start(bf16[512,2048]{1,0:T(8,128)(2,1)S(1)} %pad_maximum_fusion.k0.v0), channel_id=1, source_target_pairs={{0,2},{1,3},{2,0},{3,1},{4,6},{5,7},{6,4},{7,5},{8,10},{9,11},{10,... | collective-permute-start | bytes 6291464 | tf_op jit(solution)/shard_map/ppermute | solution.py:28
  26.3 3.0 %collective-permute-start.4 = (bf16[512,512]{1,0:T(8,128)(2,1)}, bf16[512,512]{1,0:T(8,128)(2,1)}, u32[]{:S(2)}, u32[]{:S(2)}) collective-permute-start(bf16[512,512]{1,0:T(8,128)(2,1)} %pad_maximum_fusion.3.k0.v0), channel_id=1, source_target_pairs={{0,1},{1,0},{2,3},{3,2},{4,5},{5,4},{6,7},{7,6},{8,9},{9,8},{10,11... | collective-permute-start | bytes 1572872 | tf_op jit(solution)/shard_map/ppermute | solution.py:28
  26.3 3.7 %collective-permute-start.8 = (bf16[512,512]{1,0:T(8,128)(2,1)}, bf16[512,512]{1,0:T(8,128)(2,1)}, u32[]{:S(2)}, u32[]{:S(2)}) collective-permute-start(bf16[512,512]{1,0:T(8,128)(2,1)} %collective-permute-done.5.k2.v2), channel_id=1, source_target_pairs={{0,1},{1,0},{2,3},{3,2},{4,5},{5,4},{6,7},{7,6},{8,9},{9,8},{10,11... | collective-permute-start | bytes 1572872 | tf_op jit(solution)/shard_map/ppermute | solution.py:28
  26.8 46.9 %collective-permute-start.9 = (bf16[512,2048]{1,0:T(8,128)(2,1)S(1)}, bf16[512,2048]{1,0:T(8,128)(2,1)}, u32[]{:S(2)}, u32[]{:S(2)}) collective-permute-start(bf16[512,2048]{1,0:T(8,128)(2,1)S(1)} %pad_maximum_fusion.k0.v0), channel_id=1, source_target_pairs={{0,1},{1,0},{2,3},{3,2},{4,5},{5,4},{6,7},{7,6},{8,9},{9,8},{10,11... | collective-permute-start | bytes 6291464 | tf_op jit(solution)/shard_map/ppermute | solution.py:28
  30.0 43.6 %copy-start.6 = (bf16[512,2048]{1,0:T(8,128)(2,1)S(1)}, bf16[512,2048]{1,0:T(8,128)(2,1)}, u32[]{:S(2)}) copy-start(bf16[512,2048]{1,0:T(8,128)(2,1)} %param.7) | copy-start | bytes 6291460
  72.4 4.8 %collective-permute-start.10 = (bf16[512,2048]{1,0:T(8,128)(2,1)}, bf16[512,2048]{1,0:T(8,128)(2,1)S(1)}, u32[]{:S(2)}, u32[]{:S(2)}) collective-permute-start(bf16[512,2048]{1,0:T(8,128)(2,1)} %collective-permute-done.3.k2.v2), channel_id=1, source_target_pairs={{0,1},{1,0},{2,3},{3,2},{4,5},{5,4},{6,7},{7,6},{8,9},{9,8},{10,11... | collective-permute-start | bytes 6291464 | tf_op jit(solution)/shard_map/ppermute | solution.py:28
  72.4 25.7 %collective-permute-start.2 = (bf16[512,1024]{1,0:T(8,128)(2,1)S(1)}, bf16[512,1024]{1,0:T(8,128)(2,1)}, u32[]{:S(2)}, u32[]{:S(2)}) collective-permute-start(bf16[512,1024]{1,0:T(8,128)(2,1)S(1)} %pad_maximum_fusion.1.k0.v0), channel_id=1, source_target_pairs={{0,2},{1,3},{2,0},{3,1},{4,6},{5,7},{6,4},{7,5},{8,10},{9,11},{10,... | collective-permute-start | bytes 3145736 | tf_op jit(solution)/shard_map/ppermute | solution.py:28
  73.4 29.4 %collective-permute-start.11 = (bf16[512,1024]{1,0:T(8,128)(2,1)S(1)}, bf16[512,1024]{1,0:T(8,128)(2,1)}, u32[]{:S(2)}, u32[]{:S(2)}) collective-permute-start(bf16[512,1024]{1,0:T(8,128)(2,1)S(1)} %pad_maximum_fusion.1.k0.v0), channel_id=1, source_target_pairs={{0,1},{1,0},{2,3},{3,2},{4,5},{5,4},{6,7},{7,6},{8,9},{9,8},{10,11... | collective-permute-start | bytes 3145736 | tf_op jit(solution)/shard_map/ppermute | solution.py:28
  88.2 1.0 copy-start.1
  99.8 3.0 %collective-permute-start.12 = (bf16[512,1024]{1,0:T(8,128)(2,1)}, bf16[512,1024]{1,0:T(8,128)(2,1)S(1)}, u32[]{:S(2)}, u32[]{:S(2)}) collective-permute-start(bf16[512,1024]{1,0:T(8,128)(2,1)} %collective-permute-done.2.k2.v2), channel_id=1, source_target_pairs={{0,1},{1,0},{2,3},{3,2},{4,5},{5,4},{6,7},{7,6},{8,9},{9,8},{10,11... | collective-permute-start | bytes 3145736 | tf_op jit(solution)/shard_map/ppermute | solution.py:28
  100.1 14.3 %collective-permute-start.1 = (bf16[512,512]{1,0:T(8,128)(2,1)}, bf16[512,512]{1,0:T(8,128)(2,1)S(1)}, u32[]{:S(2)}, u32[]{:S(2)}) collective-permute-start(bf16[512,512]{1,0:T(8,128)(2,1)} %pad_maximum_fusion.2.near), channel_id=1, source_target_pairs={{0,2},{1,3},{2,0},{3,1},{4,6},{5,7},{6,4},{7,5},{8,10},{9,11},{10,... | collective-permute-start | bytes 1572872 | tf_op jit(solution)/shard_map/ppermute | solution.py:28
  101.6 12.9 %collective-permute-start = (bf16[512,512]{1,0:T(8,128)(2,1)}, bf16[512,512]{1,0:T(8,128)(2,1)S(1)}, u32[]{:S(2)}, u32[]{:S(2)}) collective-permute-start(bf16[512,512]{1,0:T(8,128)(2,1)} %pad_maximum_fusion.2.near), channel_id=1, source_target_pairs={{0,1},{1,0},{2,3},{3,2},{4,5},{5,4},{6,7},{7,6},{8,9},{9,8},{10,11... | collective-permute-start | bytes 1572872 | tf_op jit(solution)/shard_map/ppermute | solution.py:28
  102.7 11.7 %copy-start.8 = (s32[32,1]{0,1:T(1,128)S(1)}, s32[32,1]{0,1:T(1,128)}, u32[]{:S(2)}) copy-start(s32[32,1]{0,1:T(1,128)} %param.13) | copy-start | bytes 388
  102.7 13.6 %copy-start = (bf16[512,4096]{1,0:T(8,128)(2,1)S(1)}, bf16[512,4096]{1,0:T(8,128)(2,1)}, u32[]{:S(2)}) copy-start(bf16[512,4096]{1,0:T(8,128)(2,1)} %refs_4_.1) | copy-start | bytes 12582916
  102.7 13.5 %copy-start.2 = (bf16[512,1024]{1,0:T(8,128)(2,1)S(1)}, bf16[512,1024]{1,0:T(8,128)(2,1)}, u32[]{:S(2)}) copy-start(bf16[512,1024]{1,0:T(8,128)(2,1)} %copy-done.1) | copy-start | bytes 3145732
  102.7 13.5 %copy-start.3 = (bf16[512,512]{1,0:T(8,128)(2,1)S(1)}, bf16[512,512]{1,0:T(8,128)(2,1)}, u32[]{:S(2)}) copy-start(bf16[512,512]{1,0:T(8,128)(2,1)} %pad_maximum_fusion.2.near) | copy-start | bytes 1572868
  102.7 13.5 %copy-start.4 = (bf16[512,256]{1,0:T(8,128)(2,1)S(1)}, bf16[512,256]{1,0:T(8,128)(2,1)}, u32[]{:S(2)}) copy-start(bf16[512,256]{1,0:T(8,128)(2,1)} %get-tuple-element.38.q) | copy-start | bytes 786436
  114.3 1.9 collective-permute-start.13
Sparse Core Ops, SparseCore 0:
  26.1 73.6 all-gather.1

commit v4 on v3

--- a/solution.py
+++ b/solution.py
@@ -12,7 +12,7 @@
 NEG_FILL = -1e30
 CHUNKS = (1, 4, 2, 1)
 Q_TILE = 256
-COL_TILE = 512
+COL_TILE = 1024
 ROW_TILE = 512
 SLOTS = 3
 MIB = 1024 * 1024
@@ -197,7 +197,7 @@
             ],
         ),
         out_shape=jax.ShapeDtypeStruct((CAP * rows, width), jnp.bfloat16),
-        compiler_params=pltpu.CompilerParams(vmem_limit_bytes=28 * MIB),
+        compiler_params=pltpu.CompilerParams(vmem_limit_bytes=40 * MIB),
         cost_estimate=pl.CostEstimate(
             flops=2 * rows * depth * width,
             bytes_accessed=2 * depth * width + 6 * rows * width,

time: 249 us -> 248 us (level)
  no operation moved by 1% of the time
where the time goes in v4:
time: 248 us
  blocking collectives  107 us (43%)
  waiting for transfers between devices  63.7 us (26%)
  Pallas kernels  40.1 us (16%)
  between operations  14.3 us (6%)
  starting transfers between devices  9.55 us (4%)
  local copies, waits for them, and re-layouts  9.1 us (4%)
  other arithmetic  4.72 us (2%)
    all_to_all x1, blocking collectives, shards(): lax.all_to_all(placed.reshape(req_count, -1, width), 'req', split_axis=0,...  107 us
    ppermute x14, waiting for transfers between devices, flip(): return lax.ppermute(x, ('req', 'ctx'), pairs)  62 us
    pallas_call x3, Pallas kernels, attend(): pl.pallas_call(attend_kernel, grid_spec=pltpu.PrefetchScalarGridSpec(num_...  21.8 us
    pallas_call x1, Pallas kernels, finish(): pl.pallas_call(finish_kernel, grid_spec=pltpu.PrefetchScalarGridSpec(num_...  14.8 us
    ppermute x14, starting transfers between devices, flip(): return lax.ppermute(x, ('req', 'ctx'), pairs)  9.55 us
    slice x7, local copies, waits for them, and re-layouts, shards(): packed.append(jnp.concatenate([keys[:, span], values[:, span]], axis=1))  5.07 us
  transfers between devices with their start and end apart: 15, of which 8 were waited for; matrix products, arithmetic and copies ran while one was open for 5% of the time, Pallas kernels for 9%

profile of v4, /device:TPU:2, one launch (start us, length us, event | category | flops | bytes accessed | tf_op | source)
XLA Modules:
  0.0 248.1 jit_solution(13921864245351187013)
XLA Ops:
  6.5 0.0 all-gather.2.cloned.1.call-start
  6.5 1.9 collective-permute-start.6
  8.5 1.3 fusion.1
  9.7 0.0 slice-start
  9.7 0.0 slice-start.1
  9.8 0.9 pad_maximum_fusion.3.k0.v0
  10.6 0.1 collective-permute-start.5
  10.7 0.2 slice-done
  11.0 0.2 slice-done.1
  11.1 0.1 pad_maximum_fusion.1.k0.v0
  11.3 0.0 copy-start.5
  11.3 0.9 pad_maximum_fusion.2.near
  12.1 2.3 slice.41
  14.5 0.0 copy-done.5
  14.5 1.1 slice.42
  15.5 0.0 collective-permute-done.6
  15.5 0.1 maximum_select_fusion.1
  15.6 3.7 %collective-permute-start.7 = (bf16[64,2048]{1,0:T(8,128)(2,1)S(1)}, bf16[64,2048]{1,0:T(8,128)(2,1)S(1)}, u32[]{:S(2)}, u32[]{:S(2)}) collective-permute-start(bf16[64,2048]{1,0:T(8,128)(2,1)S(1)} %maximum_select_fusion.1), channel_id=1, source_target_pairs={{0,18},{1,19},{2,16},{3,17},{4,22},{5,23},{6,20},{7,21},{8,26},{9,... | collective-permute-start | bytes 786440 | tf_op jit(solution)/shard_map/ppermute | solution.py:28
  19.3 1.7 pad_maximum_fusion.k0.v0
  21.0 4.0 %collective-permute-done.7 = bf16[64,2048]{1,0:T(8,128)(2,1)S(1)} collective-permute-done((bf16[64,2048]{1,0:T(8,128)(2,1)S(1)}, bf16[64,2048]{1,0:T(8,128)(2,1)S(1)}, u32[]{:S(2)}, u32[]{:S(2)}) %collective-permute-start.7) | collective-permute-done | bytes 262176 | tf_op jit(solution)/shard_map/ppermute | solution.py:28
  25.1 0.0 collective-permute-done.5.k2.v2
  25.1 0.9 maximum_select_fusion
  26.0 0.0 all-gather.2.cloned.1.call-update
  26.0 0.3 collective-permute-start.3
  26.3 0.0 collective-permute-start.4
  26.3 0.5 collective-permute-start.8
  26.8 0.0 collective-permute-start.9
  27.5 0.1 concatenate.27.meta
  27.5 1.8 fusion.3
  29.3 0.0 collective-permute-done.4.k1.v1
  29.3 0.7 collective-permute-done.8.k3.v3
  30.0 4.3 %shard_map.73.refs_0_ = bf16[512,256]{1,0:T(8,128)(2,1)S(1)} custom-call(s32[5]{0:T(128)S(1)} %concatenate.27.meta, bf16[512,256]{1,0:T(8,128)(2,1)S(1)} %get-tuple-element.37.q, bf16[512,512]{1,0:T(8,128)(2,1)} %pad_maximum_fusion.3.k0.v0, bf16[512,512]{1,0:T(8,128)(2,1)} %pad_maximum_fusion.3.k0.v0, bf16[512,512]{1,0:T(8,128)(2,1)} %collective-permute-done.4.k1.v1, ...), custom_call_target="tpu_custom_call" | custom-call | tf_op jit(solution)/shard_map/pallas_call | solution.py:81
  34.3 38.1 %collective-permute-done.3.k2.v2 = bf16[512,2048]{1,0:T(8,128)(2,1)} collective-permute-done((bf16[512,2048]{1,0:T(8,128)(2,1)S(1)}, bf16[512,2048]{1,0:T(8,128)(2,1)}, u32[]{:S(2)}, u32[]{:S(2)}) %collective-permute-start.3) | collective-permute-done | bytes 2097184 | tf_op jit(solution)/shard_map/ppermute | solution.py:28
  72.4 0.0 collective-permute-start.10
  72.4 1.0 collective-permute-start.2
  73.4 0.2 collective-permute-start.11
  73.6 0.1 slice.46.q
  73.7 0.0 collective-permute-done.9.k1.v1
  73.7 3.4 %collective-permute-done.10.k3.v3 = bf16[512,2048]{1,0:T(8,128)(2,1)S(1)} collective-permute-done((bf16[512,2048]{1,0:T(8,128)(2,1)}, bf16[512,2048]{1,0:T(8,128)(2,1)S(1)}, u32[]{:S(2)}, u32[]{:S(2)}) %collective-permute-start.10) | collective-permute-done | bytes 2097184 | tf_op jit(solution)/shard_map/ppermute | solution.py:28
  77.2 11.0 %shard_map.74.refs_1_ = bf16[512,1024]{1,0:T(8,128)(2,1)S(1)} custom-call(s32[5]{0:T(128)S(1)} %concatenate.27.meta, bf16[512,1024]{1,0:T(8,128)(2,1)S(1)} %slice.46.q, bf16[512,2048]{1,0:T(8,128)(2,1)S(1)} %pad_maximum_fusion.k0.v0, bf16[512,2048]{1,0:T(8,128)(2,1)S(1)} %pad_maximum_fusion.k0.v0, bf16[512,2048]{1,0:T(8,128)(2,1)} %collective-permute-done.9.k1.v1, ...), custom_call_target="tpu_custom_call" | custom-call | tf_op jit(solution)/shard_map/pallas_call | solution.py:81
  88.2 0.0 copy-start.1
  88.2 1.0 copy-done.1
  89.1 8.9 %collective-permute-done.2.k2.v2 = bf16[512,1024]{1,0:T(8,128)(2,1)} collective-permute-done((bf16[512,1024]{1,0:T(8,128)(2,1)S(1)}, bf16[512,1024]{1,0:T(8,128)(2,1)}, u32[]{:S(2)}, u32[]{:S(2)}) %collective-permute-start.2) | collective-permute-done | bytes 1048608 | tf_op jit(solution)/shard_map/ppermute | solution.py:28
  98.1 1.7 all-gather.2.cloned.1.call-done
  99.8 0.3 collective-permute-start.12
  100.1 1.6 collective-permute-start.1
  101.6 0.0 collective-permute-start
  101.6 1.1 slice.47.q
  102.7 0.0 copy-start.8
  102.7 0.0 copy-start
  102.7 0.0 copy-start.2
  102.7 0.0 collective-permute-done.11.k1.v1
  102.8 0.0 collective-permute-done.12.k3.v3
  102.8 6.6 %shard_map.75.refs_2_ = bf16[512,512]{1,0:T(8,128)(2,1)S(1)} custom-call(s32[5]{0:T(128)S(1)} %concatenate.27.meta, bf16[512,512]{1,0:T(8,128)(2,1)S(1)} %slice.47.q, bf16[512,1024]{1,0:T(8,128)(2,1)S(1)} %pad_maximum_fusion.1.k0.v0, bf16[512,1024]{1,0:T(8,128)(2,1)S(1)} %pad_maximum_fusion.1.k0.v0, bf16[512,1024]{1,0:T(8,128)(2,1)} %collective-permute-done.11.k1.v1, ...), custom_call_target="tpu_custom_call" | custom-call | tf_op jit(solution)/shard_map/pallas_call | solution.py:81
  109.3 5.0 %collective-permute-done.1.far = bf16[512,512]{1,0:T(8,128)(2,1)S(1)} collective-permute-done((bf16[512,512]{1,0:T(8,128)(2,1)}, bf16[512,512]{1,0:T(8,128)(2,1)S(1)}, u32[]{:S(2)}, u32[]{:S(2)}) %collective-permute-start.1) | collective-permute-done | bytes 524320 | tf_op jit(solution)/shard_map/ppermute | solution.py:28
  114.3 0.0 collective-permute-start.13
  114.3 0.0 copy-done.8
  114.4 0.2 convert_reduce_fusion
  114.5 0.0 collective-permute-done.near_beside
  114.5 1.7 collective-permute-done.13.far_beside
  116.3 0.0 copy-done.3
  116.3 14.8 %shard_map.76 = bf16[1024,4096]{1,0:T(8,128)(2,1)} custom-call(s32[5]{0:T(128)S(1)} %concatenate.27.meta, s32[32]{0:T(128)S(1)} %multiply_add_fusion.place, bf16[512,256]{1,0:T(8,128)(2,1)S(1)} %copy-done.4, bf16[512,512]{1,0:T(8,128)(2,1)S(1)} %copy-done.3, bf16[512,512]{1,0:T(8,128)(2,1)S(1)} %collective-permute-done.near_beside, ...), custom_call_target="tpu_custom_call" | custom-call | flops 8589934592 | bytes 29360128 | tf_op jit(solution)/shard_map/pallas_call | solution.py:181
  131.1 106.7 %all_to_all.5 = bf16[32,32,4096]{2,1,0:T(8,128)(2,1)S(1)} all-to-all(bf16[32,32,4096]{2,1,0:T(8,128)(2,1)} %bitcast.10), channel_id=1, replica_groups=mesh['req'=32,'ctx'=4] {'req'}, dimensions={0} | all-to-all | bytes 16777216 | tf_op jit(solution)/shard_map/all_to_all | solution.py:296
  237.8 3.4 %shard_map.77 = bf16[1024,4096]{1,0:T(8,128)(2,1)} custom-call(bf16[1024,4096]{1,0:T(8,128)(2,1)S(1)} %bitcast.9), custom_call_target="tpu_custom_call" | custom-call | tf_op jit(solution)/shard_map/pallas_call | solution.py:216
  (10 shorter events, 0.0 us)
Async XLA Ops:
  6.5 93.3 %all-gather.2.cloned.1.call-start = ((), (), s32[]{:S(2)}) async-start(), calls=%async_computation.1 | async-start | bytes 17301504 | tf_op jit(solution)/shard_map/all_gather | solution.py:257
  6.5 9.0 %collective-permute-start.6 = (bf16[64,1024]{1,0:T(8,128)(2,1)}, bf16[64,1024]{1,0:T(8,128)(2,1)S(1)}, u32[]{:S(2)}, u32[]{:S(2)}) collective-permute-start(bf16[64,1024]{1,0:T(8,128)(2,1)} %param.11), channel_id=1, source_target_pairs={{0,2},{1,3},{2,0},{3,1},{4,6},{5,7},{6,4},{7,5},{8,10},{9,11},{10,... | collective-permute-start | bytes 393224 | tf_op jit(solution)/shard_map/ppermute | solution.py:28
  9.7 1.2 slice-start
  9.7 1.4 slice-start.1
  10.6 14.5 %collective-permute-start.5 = (bf16[512,512]{1,0:T(8,128)(2,1)}, bf16[512,512]{1,0:T(8,128)(2,1)}, u32[]{:S(2)}, u32[]{:S(2)}) collective-permute-start(bf16[512,512]{1,0:T(8,128)(2,1)} %pad_maximum_fusion.3.k0.v0), channel_id=1, source_target_pairs={{0,2},{1,3},{2,0},{3,1},{4,6},{5,7},{6,4},{7,5},{8,10},{9,11},{10,... | collective-permute-start | bytes 1572872 | tf_op jit(solution)/shard_map/ppermute | solution.py:28
  11.3 3.2 %copy-start.5 = (bf16[512,2048]{1,0:T(8,128)(2,1)S(1)}, bf16[512,2048]{1,0:T(8,128)(2,1)}, u32[]{:S(2)}) copy-start(bf16[512,2048]{1,0:T(8,128)(2,1)} %param.9) | copy-start | bytes 6291460
  12.1 3.4 %copy-start.7 = (bf16[64,1024]{1,0:T(8,128)(2,1)S(1)}, bf16[64,1024]{1,0:T(8,128)(2,1)}, u32[]{:S(2)}) copy-start(bf16[64,1024]{1,0:T(8,128)(2,1)} %param.11) | copy-start | bytes 393220
  15.6 9.5 %collective-permute-start.7 = (bf16[64,2048]{1,0:T(8,128)(2,1)S(1)}, bf16[64,2048]{1,0:T(8,128)(2,1)S(1)}, u32[]{:S(2)}, u32[]{:S(2)}) collective-permute-start(bf16[64,2048]{1,0:T(8,128)(2,1)S(1)} %maximum_select_fusion.1), channel_id=1, source_target_pairs={{0,18},{1,19},{2,16},{3,17},{4,22},{5,23},{6,20},{7,21},{8,26},{9,... | collective-permute-start | bytes 786440 | tf_op jit(solution)/shard_map/ppermute | solution.py:28
  26.0 46.4 %collective-permute-start.3 = (bf16[512,2048]{1,0:T(8,128)(2,1)S(1)}, bf16[512,2048]{1,0:T(8,128)(2,1)}, u32[]{:S(2)}, u32[]{:S(2)}) collective-permute-start(bf16[512,2048]{1,0:T(8,128)(2,1)S(1)} %pad_maximum_fusion.k0.v0), channel_id=1, source_target_pairs={{0,2},{1,3},{2,0},{3,1},{4,6},{5,7},{6,4},{7,5},{8,10},{9,11},{10,... | collective-permute-start | bytes 6291464 | tf_op jit(solution)/shard_map/ppermute | solution.py:28
  26.3 3.0 %collective-permute-start.4 = (bf16[512,512]{1,0:T(8,128)(2,1)}, bf16[512,512]{1,0:T(8,128)(2,1)}, u32[]{:S(2)}, u32[]{:S(2)}) collective-permute-start(bf16[512,512]{1,0:T(8,128)(2,1)} %pad_maximum_fusion.3.k0.v0), channel_id=1, source_target_pairs={{0,1},{1,0},{2,3},{3,2},{4,5},{5,4},{6,7},{7,6},{8,9},{9,8},{10,11... | collective-permute-start | bytes 1572872 | tf_op jit(solution)/shard_map/ppermute | solution.py:28
  26.3 3.7 %collective-permute-start.8 = (bf16[512,512]{1,0:T(8,128)(2,1)}, bf16[512,512]{1,0:T(8,128)(2,1)}, u32[]{:S(2)}, u32[]{:S(2)}) collective-permute-start(bf16[512,512]{1,0:T(8,128)(2,1)} %collective-permute-done.5.k2.v2), channel_id=1, source_target_pairs={{0,1},{1,0},{2,3},{3,2},{4,5},{5,4},{6,7},{7,6},{8,9},{9,8},{10,11... | collective-permute-start | bytes 1572872 | tf_op jit(solution)/shard_map/ppermute | solution.py:28
  26.8 46.9 %collective-permute-start.9 = (bf16[512,2048]{1,0:T(8,128)(2,1)S(1)}, bf16[512,2048]{1,0:T(8,128)(2,1)}, u32[]{:S(2)}, u32[]{:S(2)}) collective-permute-start(bf16[512,2048]{1,0:T(8,128)(2,1)S(1)} %pad_maximum_fusion.k0.v0), channel_id=1, source_target_pairs={{0,1},{1,0},{2,3},{3,2},{4,5},{5,4},{6,7},{7,6},{8,9},{9,8},{10,11... | collective-permute-start | bytes 6291464 | tf_op jit(solution)/shard_map/ppermute | solution.py:28
  30.0 43.6 %copy-start.6 = (bf16[512,2048]{1,0:T(8,128)(2,1)S(1)}, bf16[512,2048]{1,0:T(8,128)(2,1)}, u32[]{:S(2)}) copy-start(bf16[512,2048]{1,0:T(8,128)(2,1)} %param.7) | copy-start | bytes 6291460
  72.4 4.8 %collective-permute-start.10 = (bf16[512,2048]{1,0:T(8,128)(2,1)}, bf16[512,2048]{1,0:T(8,128)(2,1)S(1)}, u32[]{:S(2)}, u32[]{:S(2)}) collective-permute-start(bf16[512,2048]{1,0:T(8,128)(2,1)} %collective-permute-done.3.k2.v2), channel_id=1, source_target_pairs={{0,1},{1,0},{2,3},{3,2},{4,5},{5,4},{6,7},{7,6},{8,9},{9,8},{10,11... | collective-permute-start | bytes 6291464 | tf_op jit(solution)/shard_map/ppermute | solution.py:28
  72.4 25.7 %collective-permute-start.2 = (bf16[512,1024]{1,0:T(8,128)(2,1)S(1)}, bf16[512,1024]{1,0:T(8,128)(2,1)}, u32[]{:S(2)}, u32[]{:S(2)}) collective-permute-start(bf16[512,1024]{1,0:T(8,128)(2,1)S(1)} %pad_maximum_fusion.1.k0.v0), channel_id=1, source_target_pairs={{0,2},{1,3},{2,0},{3,1},{4,6},{5,7},{6,4},{7,5},{8,10},{9,11},{10,... | collective-permute-start | bytes 3145736 | tf_op jit(solution)/shard_map/ppermute | solution.py:28
  73.4 29.4 %collective-permute-start.11 = (bf16[512,1024]{1,0:T(8,128)(2,1)S(1)}, bf16[512,1024]{1,0:T(8,128)(2,1)}, u32[]{:S(2)}, u32[]{:S(2)}) collective-permute-start(bf16[512,1024]{1,0:T(8,128)(2,1)S(1)} %pad_maximum_fusion.1.k0.v0), channel_id=1, source_target_pairs={{0,1},{1,0},{2,3},{3,2},{4,5},{5,4},{6,7},{7,6},{8,9},{9,8},{10,11... | collective-permute-start | bytes 3145736 | tf_op jit(solution)/shard_map/ppermute | solution.py:28
  88.2 1.0 copy-start.1
  99.8 3.0 %collective-permute-start.12 = (bf16[512,1024]{1,0:T(8,128)(2,1)}, bf16[512,1024]{1,0:T(8,128)(2,1)S(1)}, u32[]{:S(2)}, u32[]{:S(2)}) collective-permute-start(bf16[512,1024]{1,0:T(8,128)(2,1)} %collective-permute-done.2.k2.v2), channel_id=1, source_target_pairs={{0,1},{1,0},{2,3},{3,2},{4,5},{5,4},{6,7},{7,6},{8,9},{9,8},{10,11... | collective-permute-start | bytes 3145736 | tf_op jit(solution)/shard_map/ppermute | solution.py:28
  100.1 14.3 %collective-permute-start.1 = (bf16[512,512]{1,0:T(8,128)(2,1)}, bf16[512,512]{1,0:T(8,128)(2,1)S(1)}, u32[]{:S(2)}, u32[]{:S(2)}) collective-permute-start(bf16[512,512]{1,0:T(8,128)(2,1)} %pad_maximum_fusion.2.near), channel_id=1, source_target_pairs={{0,2},{1,3},{2,0},{3,1},{4,6},{5,7},{6,4},{7,5},{8,10},{9,11},{10,... | collective-permute-start | bytes 1572872 | tf_op jit(solution)/shard_map/ppermute | solution.py:28
  101.6 12.9 %collective-permute-start = (bf16[512,512]{1,0:T(8,128)(2,1)}, bf16[512,512]{1,0:T(8,128)(2,1)S(1)}, u32[]{:S(2)}, u32[]{:S(2)}) collective-permute-start(bf16[512,512]{1,0:T(8,128)(2,1)} %pad_maximum_fusion.2.near), channel_id=1, source_target_pairs={{0,1},{1,0},{2,3},{3,2},{4,5},{5,4},{6,7},{7,6},{8,9},{9,8},{10,11... | collective-permute-start | bytes 1572872 | tf_op jit(solution)/shard_map/ppermute | solution.py:28
  102.7 11.7 %copy-start.8 = (s32[32,1]{0,1:T(1,128)S(1)}, s32[32,1]{0,1:T(1,128)}, u32[]{:S(2)}) copy-start(s32[32,1]{0,1:T(1,128)} %param.13) | copy-start | bytes 388
  102.7 13.6 %copy-start = (bf16[512,4096]{1,0:T(8,128)(2,1)S(1)}, bf16[512,4096]{1,0:T(8,128)(2,1)}, u32[]{:S(2)}) copy-start(bf16[512,4096]{1,0:T(8,128)(2,1)} %refs_4_.1) | copy-start | bytes 12582916
  102.7 13.5 %copy-start.2 = (bf16[512,1024]{1,0:T(8,128)(2,1)S(1)}, bf16[512,1024]{1,0:T(8,128)(2,1)}, u32[]{:S(2)}) copy-start(bf16[512,1024]{1,0:T(8,128)(2,1)} %copy-done.1) | copy-start | bytes 3145732
  102.7 13.5 %copy-start.3 = (bf16[512,512]{1,0:T(8,128)(2,1)S(1)}, bf16[512,512]{1,0:T(8,128)(2,1)}, u32[]{:S(2)}) copy-start(bf16[512,512]{1,0:T(8,128)(2,1)} %pad_maximum_fusion.2.near) | copy-start | bytes 1572868
  102.7 13.5 %copy-start.4 = (bf16[512,256]{1,0:T(8,128)(2,1)S(1)}, bf16[512,256]{1,0:T(8,128)(2,1)}, u32[]{:S(2)}) copy-start(bf16[512,256]{1,0:T(8,128)(2,1)} %get-tuple-element.38.q) | copy-start | bytes 786436
  114.3 1.9 collective-permute-start.13
Sparse Core Ops, SparseCore 0:
  26.1 73.6 all-gather.1
